TPU v7x, 256 devices: a whole 4x4x8 slice. The times are simulated.
256 devices in a mesh: row: 16 (over y, x_hi, core), col: 16 (over x_lo, z).
Axes of the slice: x: 4 (x_hi: 2, x_lo: 2; x = x_hi * 2 + x_lo), y: 4, z: 8, core: 2. Of those that a mesh axis runs over, the one named last changes fastest.
Arguments:
- amplitudes: float32 [2048, 2048], P('row', 'col'), may hold values from -6 to 6
- integrals: float32 [2048, 163840], P(None, ('row', 'col')), may hold values from -3 to 3, as said below
- occ_irrep: int32 [2048], replicated, may hold values from 0 to 7, as said below
- cd_irrep: int32 [2048], P('col'), may hold values from 0 to 7
- vir_irrep: int32 [163840], P(('row', 'col')), may hold values from 0 to 7, as said below
- occ_energy: float32 [2048], replicated, may hold values from -4 to -1, as said below
- vir_energy: float32 [163840], P(('row', 'col')), may hold values from 1 to 6, as said below
Outputs:
- update: float32 [2048, 163840], P(None, ('row', 'col'))
Inputs may be any that keep to these rules, and one draw needn't show every extreme that they name: `occ_irrep`: entry p equals entry p + 2048/2 (a pair and its mirror share their irrep). `vir_irrep`: entry q equals entry q + 81920. `occ_energy`: entry p equals entry p + 1024. `vir_energy`: entry q equals entry q + 81920. `integrals`: column q + 81920 is exactly minus column q (antisymmetry in ab).
All inputs are finite; a program needn't handle non-finite values.
Results may differ from a plain program's by a relative error of at most 0.000088.
Values sent between devices are 32-bit elements; how exact they have to be, the bound alone decides.
No kernel may reach another device: no remote copies, remote signals or barrier semaphores. Data moves between devices by JAX's collectives and lax.ppermute only.
A program may use at most 128 MiB of HBM per device.

v0:
```python
import functools

import jax
import jax.numpy as jnp
from jax import lax
from jax.experimental import pallas as pl
from jax.experimental.pallas import tpu as pltpu
from jax.sharding import Mesh
from jax.sharding import PartitionSpec as P

BLOCK = 128
IRREPS = 8
HALF = 16
META = 8
SLOTS = 2 * HALF
BLOCKS = 8
COLS = 16
PART = BLOCKS // 2
SPLIT = 2

ROW = ("yh", "yl", "xh", "core")
COL = ("xl", "z2", "z1", "z0")

NEAR = ("yh", "yl", "xl")
COL_STEPS = (("z2", "z1"), ("z1",), ("z0",))
X_STEP = ("xh", "xl")

f32, bf16, i32 = jnp.float32, jnp.bfloat16, jnp.int32
MIB = 1 << 20


def iota(shape, dim):
    return lax.broadcasted_iota(i32, shape, dim)


def strict_upper():
    return jnp.where(iota((BLOCK, BLOCK), 0) < iota((BLOCK, BLOCK), 1), 1.0, 0.0).astype(bf16)


def mm(a, b):
    return jnp.dot(a, b, preferred_element_type=f32)


def high_low(x):
    high = x.astype(bf16)
    return high, (x - high.astype(f32)).astype(bf16)


def number(axes):
    total = 0
    for axis in axes:
        total = 2 * total + lax.axis_index(axis)
    return total


def own_block():
    return number(ROW[1:])


def other_block(index):
    xh = lax.axis_index("xh") ^ (index >> 2)
    core = lax.axis_index("core") ^ (index >> 1 & 1)
    return (index & 1) * 4 + xh * 2 + core


def other_col(index):
    mask = 0
    for place, step in enumerate(COL_STEPS):
        if index >> 1 + place & 1:
            mask ^= sum(1 << (len(COL) - 1 - COL.index(axis)) for axis in step)
    return (index & 1) * 8 + (number(COL[1:]) ^ mask)


def rank_of(slot, upper):
    return 2 * slot + upper


def flat(ref):
    return jnp.concatenate([ref[i : i + 1, :] for i in range(ref.shape[0])], axis=1)


def pack_kernel(base_ref, amp_ref, occ_ref, cd_ref, out_ref):
    upper = lax.axis_index("yh")
    y = number(("yh", "yl"))
    occ = occ_ref[pl.ds(own_block(), 1), :]
    same = jnp.where(occ == iota((IRREPS, BLOCK), 0), 1.0, 0.0)
    ranks = mm(same.astype(bf16), strict_upper())
    rank = jnp.sum(same * ranks, axis=0, keepdims=True).astype(i32)
    key = occ * BLOCK + rank - base_ref[0] * SLOTS
    line = iota((2 * BLOCK, BLOCK), 0)
    wanted = ((line >> 4) & 7) * BLOCK + rank_of(line & 15, line >> 7)
    pick = jnp.where(key == wanted, 1.0, 0.0).astype(bf16)
    amp = amp_ref[...]
    first = amp.astype(bf16)
    rest = amp - first.astype(f32)
    second = rest.astype(bf16)
    third = (rest - second.astype(f32)).astype(bf16)
    packed = mm(pick, first) + mm(pick, second) + mm(pick, third)
    cd = cd_ref[...]
    sign = (1 - 2 * upper).astype(f32)
    tile = jnp.where(iota((META, BLOCK), 0) == number(COL[1:]), cd.astype(f32), 0.0)
    for side in range(2):
        total = jnp.zeros((HALF, BLOCK), f32)
        for g in range(IRREPS):
            lines = packed[side * BLOCK + g * HALF : side * BLOCK + (g + 1) * HALF]
            total = total + jnp.where(cd == g, lines, 0.0)
        total = sign * total
        for yl in range(2):
            mine = jnp.where(y == 2 * side + yl, tile, 0.0)
            for xl in range(2):
                place = 4 * side + 2 * yl + xl
                out_ref[place, :HALF, :] = total
                out_ref[place, HALF:, :] = mine


def table_kernel(
    base_ref, occ_ref, energy_ref, vir_ref, vir_energy_ref, scale_ref, rows_ref, token_ref, passes_ref
):
    token_ref[...] = jnp.zeros(token_ref.shape, f32)
    upper = lax.axis_index("yh")

    def ordered(ref):
        return jnp.concatenate(
            [ref[pl.ds(other_block(i), 1), :] for i in range(BLOCKS)], axis=0
        )

    occ = ordered(occ_ref)
    energy = ordered(energy_ref)
    irrep = iota((IRREPS, BLOCK), 0)
    same = jnp.concatenate(
        [jnp.where(occ[b : b + 1] == irrep, 1.0, 0.0) for b in range(BLOCKS)], axis=0
    )
    ranks = mm(same.astype(bf16), strict_upper())
    counts = jnp.sum(same, axis=1, keepdims=True)
    most = jnp.max(counts).astype(i32)
    passes_ref[0] = (most + SLOTS - 1) // SLOTS
    rank = jnp.concatenate(
        [
            jnp.sum((same * ranks)[b * IRREPS : (b + 1) * IRREPS], axis=0, keepdims=True)
            for b in range(BLOCKS)
        ],
        axis=0,
    ).astype(i32) - base_ref[0] * SLOTS
    both = jnp.concatenate(
        [occ.astype(f32), rank.astype(f32), jnp.zeros((BLOCK - 2 * BLOCKS, BLOCK), f32)], axis=0
    )
    rows_ref[...] = both.T
    key = occ * BLOCK + rank
    line = iota((BLOCK, BLOCK), 0)
    wanted = (line >> 4) * BLOCK + rank_of(line & 15, upper)
    vir = flat(vir_ref)
    vir_energy = flat(vir_energy_ref)
    for b in range(BLOCKS):
        found = jnp.sum(
            jnp.where(key[b : b + 1] == wanted, energy[b : b + 1], 0.0), axis=1, keepdims=True
        )
        at_slot = jnp.zeros((HALF, vir.shape[1]), f32)
        for g in range(IRREPS):
            at_slot = at_slot + jnp.where(vir == g, found[g * HALF : (g + 1) * HALF], 0.0)
        scale_ref[b * HALF : (b + 1) * HALF, :] = 0.5 / (at_slot - vir_energy)


def load_kernel(v_ref, out_ref, token_ref, sems):
    token_ref[...] = jnp.zeros(token_ref.shape, f32)
    copies = []
    for j in range(COLS):
        start = pl.multiple_of(other_col(j) * BLOCK, BLOCK)
        copies.append(pltpu.make_async_copy(v_ref.at[pl.ds(start, BLOCK)], out_ref.at[j], sems.at[j]))
        copies[-1].start()
    for copy in copies:
        copy.wait()


def split_kernel(part, meta_ref, vir_ref, held_ref, high_ref, low_ref, token_ref):
    token_ref[...] = jnp.zeros(token_ref.shape, f32)
    columns = range(part * (COLS // 2), (part + 1) * (COLS // 2))
    meta = jnp.concatenate(
        [meta_ref[pl.ds(other_col(j), 1), :] for j in columns]
        + [jnp.zeros((BLOCK - COLS // 2, BLOCK), f32)],
        axis=0,
    ).T
    vir = flat(vir_ref).astype(f32)
    for place, j in enumerate(columns):
        high, low = high_low(jnp.where(meta[:, place : place + 1] == vir, held_ref[j], 0.0))
        high_ref[place * BLOCK : (place + 1) * BLOCK, :] = high
        low_ref[place * BLOCK : (place + 1) * BLOCK, :] = low


def places(j):
    return [(j >> 1) * 4 + 2 * yl + (j & 1) for yl in range(2)]


def ladder_kernel(side, near_ref, *refs):
    far_refs, (high_refs, low_refs) = refs[:SPLIT], (refs[SPLIT : SPLIT + 4 : 2], refs[SPLIT + 1 : SPLIT + 4 : 2])
    scale_ref, out_ref, *token_ref = refs[SPLIT + 4 :]
    step = 2 * COLS // SPLIT
    for ref in token_ref:
        ref[...] = jnp.zeros(ref.shape, f32)
    lines = PART * HALF
    total = None
    group = 4
    for j0 in range(0, COLS, group):
        left = [
            jnp.concatenate(
                [near_ref[e] for e in places(j)]
                + [far_refs[e // step][e % step] for e in places(j)],
                axis=0,
            )
            for j in range(j0, j0 + group)
        ]
        part, first = divmod(j0, COLS // 2)
        depth = slice(first * BLOCK, (first + group) * BLOCK)
        a_high, a_low = high_low(jnp.concatenate(left, axis=1))
        twice = mm(jnp.concatenate([a_high, a_low], axis=0), high_refs[part][depth, :])
        term = twice[:lines] + twice[lines:] + mm(a_high, low_refs[part][depth, :])
        total = term if total is None else total + term
    out_ref[...] = total * scale_ref[side * lines : (side + 1) * lines, :]


def expand_kernel(side, own_ref, other_ref, rows_ref, vir_ref, *refs):
    out_ref, held, sems = refs[-3:]
    upper = lax.axis_index("yh")
    lane = iota((1, 2 * SLOTS), 1)
    mine = (lane & HALF) == 0
    wanted = rank_of(lane & 15, jnp.where(mine, upper, 1 - upper)).astype(f32)
    sign = jnp.where(mine, 1.0, -1.0)
    vir = flat(vir_ref).astype(f32)
    copies = []
    for r in range(PART):
        slots = slice(r * HALF, (r + 1) * HALF)
        i = side * PART + r
        packed = jnp.concatenate([own_ref[slots, :], other_ref[slots, :]], axis=0)
        high, low = high_low(packed)
        pick = jnp.where(rows_ref[:, BLOCKS + i : BLOCKS + i + 1] == wanted, sign, 0.0).astype(bf16)
        spread = mm(pick, jnp.concatenate([high, low], axis=0))
        spread = jnp.where(rows_ref[:, i : i + 1] == vir, spread, 0.0)
        held[0, r] = spread
        held[1, r] = -spread
        for mirror in range(2):
            copies.append(
                pltpu.make_async_copy(
                    held.at[mirror, r], out_ref.at[mirror, other_block(i)], sems.at[mirror, r]
                )
            )
            copies[-1].start()
    for copy in copies:
        copy.wait()


def join_kernel(in_ref, after_ref, out_ref):
    pass


VMEM = pl.BlockSpec(memory_space=pltpu.VMEM)
SMEM = pl.BlockSpec(memory_space=pltpu.SMEM)
ANY = pl.BlockSpec(memory_space=pl.ANY)
HBM = pl.BlockSpec(memory_space=pltpu.HBM)


SMALL = pl.CostEstimate(flops=1000, bytes_accessed=1000, transcendentals=0)


def params(mib):
    return pltpu.CompilerParams(vmem_limit_bytes=mib * MIB)


def swapped(x, *axes):
    axes = tuple(sorted(axes, key=(ROW + COL).index))
    count = 1 << len(axes)
    return lax.ppermute(x, axes, [(i, count - 1 - i) for i in range(count)])


def core_swapped(x, token=None):
    parts = jnp.split(x, SPLIT)
    if token is not None:
        parts = [jnp.concatenate([part, token], axis=0) for part in parts]
    return [swapped(part, "core") for part in parts]


def one_pass(base, amplitudes, integrals, occ, cd, vir, energy, vir_energy):
    depth, width = integrals.shape
    shape = jax.ShapeDtypeStruct
    token = shape((1, HALF, BLOCK), f32)
    packed = pl.pallas_call(
        pack_kernel,
        out_shape=shape((8, HALF + META, BLOCK), f32),
        in_specs=[SMEM, VMEM, VMEM, VMEM],
        out_specs=VMEM,
        compiler_params=params(8),
    )(base, amplitudes, occ, cd)
    scale, rows, listed, passes = pl.pallas_call(
        table_kernel,
        out_shape=[
            shape((BLOCKS * HALF, width), f32),
            shape((BLOCK, BLOCK), f32),
            token,
            shape((1,), i32),
        ],
        in_specs=[SMEM, VMEM, VMEM, VMEM, VMEM],
        out_specs=[VMEM, VMEM, VMEM, SMEM],
        compiler_params=params(8),
        cost_estimate=SMALL,
    )(base, occ, energy, vir, vir_energy)

    v, loaded = pl.pallas_call(
        load_kernel,
        out_shape=[shape((COLS, BLOCK, width), f32), token],
        in_specs=[HBM],
        out_specs=[VMEM] * 2,
        scratch_shapes=[pltpu.SemaphoreType.DMA((COLS,))],
        compiler_params=params(8),
        cost_estimate=SMALL,
    )(integrals)

    met = lax.all_to_all(packed, NEAR, 0, 0, tiled=True)
    met = met[:4] + met[4:]
    x = met[:, :HALF].reshape(-1, BLOCK)
    meta = (met[:2, HALF:] + met[2:, HALF:]).reshape(-1, BLOCK)
    def split(part, meta):
        return pl.pallas_call(
            functools.partial(split_kernel, part),
            out_shape=[shape((depth // 2, width), bf16), shape((depth // 2, width), bf16), token],
            in_specs=[VMEM] * 3,
            out_specs=[VMEM] * 3,
            compiler_params=params(24),
            cost_estimate=SMALL,
        )(meta, vir, v)

    for step, token_done in zip(COL_STEPS, (listed, loaded, None)):
        there = swapped(jnp.concatenate([x, meta], axis=0), *step)
        meta = meta + there[x.shape[0] :]
        x = jnp.concatenate([x, there[: x.shape[0]]], axis=0)
        if token_done is not None:
            known = meta
            meta = meta + token_done[0]
    x = x.reshape(-1, HALF, BLOCK)
    *early, early_token = split(0, known)
    beyond = swapped(jnp.concatenate([x, early_token], axis=0), *X_STEP)[:-1]
    near = core_swapped(x)
    *late, late_token = split(1, meta)

    def ladder(side, near, far):
        return pl.pallas_call(
            functools.partial(ladder_kernel, side),
            out_shape=[shape((PART * HALF, width), f32)] + [token] * (1 - side),
            in_specs=[VMEM] * (6 + SPLIT),
            out_specs=[VMEM] * (2 - side),
            compiler_params=params(24),
            cost_estimate=SMALL,
        )(near, *far, *early, *late, scale)

    def expand(side, own, other, *out):
        return pl.pallas_call(
            functools.partial(expand_kernel, side),
            out_shape=pltpu.HBM((2, BLOCKS, BLOCK, width), f32),
            in_specs=[VMEM] * 4 + [HBM] * len(out),
            out_specs=HBM,
            scratch_shapes=[
                pltpu.VMEM((2, PART, BLOCK, width), f32),
                pltpu.SemaphoreType.DMA((2, PART)),
            ],
            input_output_aliases={4: 0} if out else {},
            compiler_params=params(24),
            cost_estimate=SMALL,
        )(own, other, rows, vir, *out)

    first, done = ladder(0, x, near)
    first_met = swapped(first, "yh")
    (second,) = ladder(1, beyond, core_swapped(beyond, done + late_token))
    second = pl.pallas_call(
        join_kernel,
        out_shape=shape(second.shape, f32),
        in_specs=[ANY, ANY],
        out_specs=ANY,
        input_output_aliases={0: 0},
        compiler_params=params(8),
        cost_estimate=SMALL,
    )(second, first_met)
    second_met = swapped(second, "yh")
    out = expand(0, first, first_met)
    out = expand(1, second, second_met, out)
    return out, passes[0]


def local(amplitudes, integrals, occ_irrep, cd_irrep, vir_irrep, occ_energy, vir_energy):
    run = functools.partial(
        one_pass,
        amplitudes=amplitudes,
        integrals=integrals,
        occ=occ_irrep.reshape(-1, BLOCK),
        cd=cd_irrep.reshape(1, -1),
        vir=vir_irrep.reshape(-1, BLOCK),
        energy=occ_energy.reshape(-1, BLOCK),
        vir_energy=vir_energy.reshape(-1, BLOCK),
    )
    out, passes = run(jnp.zeros((1,), i32))

    def step(state):
        index, total = state
        extra, _ = run(jnp.full((1,), index, i32))
        return index + 1, total + extra

    def further(total):
        return lax.while_loop(lambda state: state[0] < passes, step, (jnp.int32(1), total))[1]

    out = lax.cond(passes > 1, further, lambda total: total, out)
    return out.reshape(occ_irrep.shape[0], -1)


def solution(mesh):
    bits = Mesh(mesh.devices.reshape((2,) * 8), ROW + COL)
    in_specs = (
        P(ROW, COL),
        P(None, ROW + COL),
        P(),
        P(COL),
        P(ROW + COL),
        P(),
        P(ROW + COL),
    )
    out_specs = P(None, ROW + COL)
    return jax.shard_map(local, mesh=bits, in_specs=in_specs, out_specs=out_specs, check_vma=False)
```

profile of v0, /device:TPU:1, one launch (start us, length us, event | category | flops | bytes accessed | tf_op | source)
XLA Modules:
  0.0 54.7 jit_solution(2459528119883249730)
XLA Ops:
  0.0 0.0 copy-start.1
  0.0 1.2 %shard_map.76 = f32[8,24,128]{2,1,0:T(8,128)S(1)} custom-call(s32[1]{0:T(128)} %constant.2.clone.1.base_ref, f32[128,128]{1,0:T(8,128)} %amp_ref.1, s32[16,128]{1,0:T(8,128)} %bitcast.77, s32[1,128]{1,0:T(1,128)} %bitcast.86), custom_call_target="tpu_custom_call" | custom-call | tf_op jit(solution)/shard_map/pallas_call | solution.py:284
  1.2 11.1 %all_to_all.11 = f32[8,24,128]{2,1,0:T(8,128)S(1)} all-to-all(f32[8,24,128]{2,1,0:T(8,128)S(1)} %shard_map.76), channel_id=1, replica_groups=mesh['yh'=2,'yl'=2,'xh'=2,'core'=2,'xl'=2,'z2'=2,'z1'=2,'z0'=2] {'yh','y..., dimensions={0} | all-to-all | bytes 196608 | tf_op jit(solution)/shard_map/all_to_all | solution.py:315
  12.4 6.1 %collective-permute-start.10 = (f32[80,128]{1,0:T(8,128)S(1)}, f32[80,128]{1,0:T(8,128)S(1)}, u32[]{:S(2)}, u32[]{:S(2)}) collective-permute-start(f32[80,128]{1,0:T(8,128)S(1)} %pad_maximum_fusion.15), channel_id=1, source_target_pairs={{0,6},{2,4},{4,2},{6,0},{1,7},{3,5},{5,3},{7,1},{8,14},{10,12},{12... | collective-permute-start | bytes 122888 | tf_op jit(solution)/shard_map/ppermute | solution.py:270
  18.5 1.5 %shard_map.75 = (f32[128,640]{1,0:T(8,128)S(1)}, f32[128,128]{1,0:T(8,128)S(1)}, f32[1,16,128]{2,1,0:T(8,128)S(1)}, s32[1]{0:T(128)}) custom-call(s32[1]{0:T(128)} %constant.2.clone.1.base_ref, s32[16,128]{1,0:T(8,128)} %bitcast.78, f32[16,128]{1,0:T(8,128)} %bitcast.81, s32[5,128]{1,0:T(8,128)} %bitcast.65, f32[5,128]{1,0:T(8,128)} %bitcast.83), custom_call_target="tpu_custom_call" | custom-call | flops 1000 | bytes 1000 | tf_op jit(solution)/shard_map/pallas_call | solution.py:291
  20.0 0.0 collective-permute-done.10
  20.0 1.3 %collective-permute-start.11 = (f32[144,128]{1,0:T(8,128)S(1)}, f32[144,128]{1,0:T(8,128)S(1)}, u32[]{:S(2)}, u32[]{:S(2)}) collective-permute-start(f32[144,128]{1,0:T(8,128)S(1)} %pad_maximum_fusion.14), channel_id=1, source_target_pairs={{0,2},{2,0},{1,3},{3,1},{4,6},{6,4},{5,7},{7,5},{8,10},{10,8},{9,1... | collective-permute-start | bytes 221192 | tf_op jit(solution)/shard_map/ppermute | solution.py:270
  21.3 2.6 %shard_map.77 = (f32[16,128,640]{2,1,0:T(8,128)S(1)}, f32[1,16,128]{2,1,0:T(8,128)S(1)}) custom-call(f32[2048,640]{1,0:T(8,128)} %v_ref.1), custom_call_target="tpu_custom_call" | custom-call | flops 1000 | bytes 1000 | tf_op jit(solution)/shard_map/pallas_call | solution.py:305
  23.9 1.1 %collective-permute-done.11 = f32[144,128]{1,0:T(8,128)S(1)} collective-permute-done((f32[144,128]{1,0:T(8,128)S(1)}, f32[144,128]{1,0:T(8,128)S(1)}, u32[]{:S(2)}, u32[]{:S(2)}) %collective-permute-start.11) | collective-permute-done | bytes 73760 | tf_op jit(solution)/shard_map/ppermute | solution.py:270
  25.1 0.1 collective-permute-start.12
  25.2 0.0 copy-done.1
  25.2 0.6 %shard_map.78 = (bf16[1024,640]{1,0:T(8,128)(2,1)S(1)}, bf16[1024,640]{1,0:T(8,128)(2,1)S(1)}, f32[1,16,128]{2,1,0:T(8,128)S(1)}) custom-call(f32[16,128]{1,0:T(8,128)S(1)} %get-tuple-element.156.meta_ref, s32[5,128]{1,0:T(8,128)S(1)} %bitcast.66, f32[16,128,640]{2,1,0:T(8,128)S(1)} %get-tuple-element.121.held_ref), custom_call_target="tpu_custom_call" | custom-call | flops 1000 | bytes 1000 | tf_op jit(solution)/shard_map/pallas_call | solution.py:320
  25.8 3.5 %collective-permute-done.12 = f32[272,128]{1,0:T(8,128)S(1)} collective-permute-done((f32[272,128]{1,0:T(8,128)S(1)}, f32[272,128]{1,0:T(8,128)S(1)}, u32[]{:S(2)}, u32[]{:S(2)}) %collective-permute-start.12) | collective-permute-done | bytes 139296 | tf_op jit(solution)/shard_map/ppermute | solution.py:270
  29.4 1.8 %collective-permute-start.13 = (f32[33,16,128]{2,1,0:T(8,128)S(1)}, f32[33,16,128]{2,1,0:T(8,128)S(1)}, u32[]{:S(2)}, u32[]{:S(2)}) collective-permute-start(f32[33,16,128]{2,1,0:T(8,128)S(1)} %pad_maximum_fusion.8), channel_id=1, source_target_pairs={{0,40},{8,32},{32,8},{40,0},{1,41},{9,33},{33,9},{41,1},{2,42},{10... | collective-permute-start | bytes 811016 | tf_op jit(solution)/shard_map/ppermute | solution.py:270
  31.2 5.4 %collective-permute-start.14 = (f32[16,16,128]{2,1,0:T(8,128)S(1)}, f32[16,16,128]{2,1,0:T(8,128)S(1)}, u32[]{:S(2)}, u32[]{:S(2)}) collective-permute-start(f32[16,16,128]{2,1,0:T(8,128)S(1)} %bitcast.85), channel_id=1, source_target_pairs={{0,16},{16,0},{1,17},{17,1},{2,18},{18,2},{3,19},{19,3},{4,20},{20... | collective-permute-start | bytes 393224 | tf_op jit(solution)/shard_map/ppermute | solution.py:270
  36.6 0.1 collective-permute-start.15
  36.7 0.6 %shard_map.79 = (bf16[1024,640]{1,0:T(8,128)(2,1)S(1)}, bf16[1024,640]{1,0:T(8,128)(2,1)S(1)}, f32[1,16,128]{2,1,0:T(8,128)S(1)}) custom-call(f32[16,128]{1,0:T(8,128)S(1)} %slice_add_fusion.6.meta_ref, s32[5,128]{1,0:T(8,128)S(1)} %bitcast.67, f32[16,128,640]{2,1,0:T(8,128)S(1)} %get-tuple-element.121.held_ref), custom_call_target="tpu_custom_call" | custom-call | flops 1000 | bytes 1000 | tf_op jit(solution)/shard_map/pallas_call | solution.py:320
  37.3 0.2 collective-permute-done.14.refs_0_
  37.5 0.4 collective-permute-done.15.refs_1_
  37.9 1.0 %shard_map.80 = (f32[64,640]{1,0:T(8,128)S(1)}, f32[1,16,128]{2,1,0:T(8,128)S(1)}) custom-call(f32[32,16,128]{2,1,0:T(8,128)S(1)} %bitcast.54, f32[16,16,128]{2,1,0:T(8,128)S(1)} %collective-permute-done.14.refs_0_, f32[16,16,128]{2,1,0:T(8,128)S(1)} %collective-permute-done.15.refs_1_, bf16[1024,640]{1,0:T(8,128)(2,1)S(1)} %get-tuple-element.123.refs_2_, ...), custom_call_target="tpu_custom_call" | custom-call | flops 1000 | bytes 1000 | tf_op jit(solution)/shard_map/pallas_call | solution.py:343
  38.9 0.7 %collective-permute-start.18 = (f32[64,640]{1,0:T(8,128)S(1)}, f32[64,640]{1,0:T(8,128)S(1)}, u32[]{:S(2)}, u32[]{:S(2)}) collective-permute-start(f32[64,640]{1,0:T(8,128)S(1)} %get-tuple-element.130.own_ref), channel_id=1, source_target_pairs={{0,128},{128,0},{1,129},{129,1},{2,130},{130,2},{3,131},{131,3},{4... | collective-permute-start | bytes 491528 | tf_op jit(solution)/shard_map/ppermute | solution.py:270
  39.7 0.0 collective-permute-done.13
  39.7 2.6 %collective-permute-start.17 = (f32[17,16,128]{2,1,0:T(8,128)S(1)}, f32[17,16,128]{2,1,0:T(8,128)S(1)}, u32[]{:S(2)}, u32[]{:S(2)}) collective-permute-start(f32[17,16,128]{2,1,0:T(8,128)S(1)} %get-tuple-element.163), channel_id=1, source_target_pairs={{0,16},{16,0},{1,17},{17,1},{2,18},{18,2},{3,19},{19,3},{4,20},{20... | collective-permute-start | bytes 417800 | tf_op jit(solution)/shard_map/ppermute | solution.py:270
  42.3 0.1 collective-permute-start.16
  42.4 0.9 %collective-permute-done.17.refs_1_ = f32[17,16,128]{2,1,0:T(8,128)S(1)} collective-permute-done((f32[17,16,128]{2,1,0:T(8,128)S(1)}, f32[17,16,128]{2,1,0:T(8,128)S(1)}, u32[]{:S(2)}, u32[]{:S(2)}) %collective-permute-start.17) | collective-permute-done | bytes 139296 | tf_op jit(solution)/shard_map/ppermute | solution.py:270
  43.3 0.4 collective-permute-done.16.refs_0_
  43.6 1.0 %shard_map.81.in_ref = f32[64,640]{1,0:T(8,128)S(1)} custom-call(f32[32,16,128]{2,1,0:T(8,128)S(1)} %slice.116.near_ref, f32[17,16,128]{2,1,0:T(8,128)S(1)} %collective-permute-done.16.refs_0_, f32[17,16,128]{2,1,0:T(8,128)S(1)} %collective-permute-done.17.refs_1_, bf16[1024,640]{1,0:T(8,128)(2,1)S(1)} %get-tuple-element.123.refs_2_, ...), custom_call_target="tpu_custom_call" | custom-call | flops 1000 | bytes 1000 | tf_op jit(solution)/shard_map/pallas_call | solution.py:343
  44.7 1.5 %collective-permute-done.18.after_ref.other_ref = f32[64,640]{1,0:T(8,128)S(1)} collective-permute-done((f32[64,640]{1,0:T(8,128)S(1)}, f32[64,640]{1,0:T(8,128)S(1)}, u32[]{:S(2)}, u32[]{:S(2)}) %collective-permute-start.18) | collective-permute-done | bytes 163872 | tf_op jit(solution)/shard_map/ppermute | solution.py:270
  46.2 0.6 %collective-permute-start.19 = (f32[64,640]{1,0:T(8,128)S(1)}, f32[64,640]{1,0:T(8,128)S(1)}, u32[]{:S(2)}, u32[]{:S(2)}) collective-permute-start(f32[64,640]{1,0:T(8,128)S(1)} %shard_map.82.own_ref), channel_id=1, source_target_pairs={{0,128},{128,0},{1,129},{129,1},{2,130},{130,2},{3,131},{131,3},{4... | collective-permute-start | bytes 491528 | tf_op jit(solution)/shard_map/ppermute | solution.py:270
  47.4 1.8 %shard_map.83.refs_0_ = f32[2,8,128,640]{3,2,1,0:T(8,128)} custom-call(f32[64,640]{1,0:T(8,128)S(1)} %get-tuple-element.130.own_ref, f32[64,640]{1,0:T(8,128)S(1)} %collective-permute-done.18.after_ref.other_ref, f32[128,128]{1,0:T(8,128)S(1)} %get-tuple-element.131.rows_ref, s32[5,128]{1,0:T(8,128)S(1)} %bitcast.68), custom_call_target="tpu_custom_call" | custom-call | flops 1000 | bytes 1000 | tf_op jit(solution)/shard_map/pallas_call | solution.py:353
  49.2 0.0 copy-start.2
  49.2 0.0 copy-start.3
  49.2 0.0 copy-start.4
  49.2 0.0 copy-start.5
  49.2 0.0 copy-start.6
  49.2 3.1 %collective-permute-done.19.other_ref = f32[64,640]{1,0:T(8,128)S(1)} collective-permute-done((f32[64,640]{1,0:T(8,128)S(1)}, f32[64,640]{1,0:T(8,128)S(1)}, u32[]{:S(2)}, u32[]{:S(2)}) %collective-permute-start.19) | collective-permute-done | bytes 163872 | tf_op jit(solution)/shard_map/ppermute | solution.py:270
  52.4 1.8 %shard_map.84 = f32[2,8,128,640]{3,2,1,0:T(8,128)} custom-call(f32[64,640]{1,0:T(8,128)S(1)} %shard_map.82.own_ref, f32[64,640]{1,0:T(8,128)S(1)} %collective-permute-done.19.other_ref, f32[128,128]{1,0:T(8,128)S(1)} %get-tuple-element.131.rows_ref, s32[5,128]{1,0:T(8,128)S(1)} %bitcast.69, ...), custom_call_target="tpu_custom_call", output_to_operand_aliasing={{}: (4, {})} | custom-call | flops 1000 | bytes 1000 | tf_op jit(solution)/shard_map/pallas_call | solution.py:353
  54.2 0.0 copy-done.2
  54.2 0.0 copy-done.3
  54.2 0.0 copy-done.4
  54.2 0.0 copy-done.5
  54.2 0.0 copy-done.6
  54.2 0.2 conditional.1
  (20 shorter events, 0.2 us)
Async XLA Ops:
  0.0 25.2 %copy-start.1 = (s32[640]{0:T(1024)S(1)}, s32[640]{0:T(1024)}, u32[]{:S(2)}) copy-start(s32[640]{0:T(1024)} %param.15) | copy-start | bytes 7684
  12.4 7.6 %collective-permute-start.10 = (f32[80,128]{1,0:T(8,128)S(1)}, f32[80,128]{1,0:T(8,128)S(1)}, u32[]{:S(2)}, u32[]{:S(2)}) collective-permute-start(f32[80,128]{1,0:T(8,128)S(1)} %pad_maximum_fusion.15), channel_id=1, source_target_pairs={{0,6},{2,4},{4,2},{6,0},{1,7},{3,5},{5,3},{7,1},{8,14},{10,12},{12... | collective-permute-start | bytes 122888 | tf_op jit(solution)/shard_map/ppermute | solution.py:270
  20.0 5.0 %collective-permute-start.11 = (f32[144,128]{1,0:T(8,128)S(1)}, f32[144,128]{1,0:T(8,128)S(1)}, u32[]{:S(2)}, u32[]{:S(2)}) collective-permute-start(f32[144,128]{1,0:T(8,128)S(1)} %pad_maximum_fusion.14), channel_id=1, source_target_pairs={{0,2},{2,0},{1,3},{3,1},{4,6},{6,4},{5,7},{7,5},{8,10},{10,8},{9,1... | collective-permute-start | bytes 221192 | tf_op jit(solution)/shard_map/ppermute | solution.py:270
  25.1 4.2 %collective-permute-start.12 = (f32[272,128]{1,0:T(8,128)S(1)}, f32[272,128]{1,0:T(8,128)S(1)}, u32[]{:S(2)}, u32[]{:S(2)}) collective-permute-start(f32[272,128]{1,0:T(8,128)S(1)} %pad_maximum_fusion.12), channel_id=1, source_target_pairs={{0,1},{1,0},{2,3},{3,2},{4,5},{5,4},{6,7},{7,6},{8,9},{9,8},{10,11... | collective-permute-start | bytes 417800 | tf_op jit(solution)/shard_map/ppermute | solution.py:270
  29.4 10.3 %collective-permute-start.13 = (f32[33,16,128]{2,1,0:T(8,128)S(1)}, f32[33,16,128]{2,1,0:T(8,128)S(1)}, u32[]{:S(2)}, u32[]{:S(2)}) collective-permute-start(f32[33,16,128]{2,1,0:T(8,128)S(1)} %pad_maximum_fusion.8), channel_id=1, source_target_pairs={{0,40},{8,32},{32,8},{40,0},{1,41},{9,33},{33,9},{41,1},{2,42},{10... | collective-permute-start | bytes 811016 | tf_op jit(solution)/shard_map/ppermute | solution.py:270
  31.2 6.4 %collective-permute-start.14 = (f32[16,16,128]{2,1,0:T(8,128)S(1)}, f32[16,16,128]{2,1,0:T(8,128)S(1)}, u32[]{:S(2)}, u32[]{:S(2)}) collective-permute-start(f32[16,16,128]{2,1,0:T(8,128)S(1)} %bitcast.85), channel_id=1, source_target_pairs={{0,16},{16,0},{1,17},{17,1},{2,18},{18,2},{3,19},{19,3},{4,20},{20... | collective-permute-start | bytes 393224 | tf_op jit(solution)/shard_map/ppermute | solution.py:270
  36.6 1.3 %collective-permute-start.15 = (f32[16,16,128]{2,1,0:T(8,128)S(1)}, f32[16,16,128]{2,1,0:T(8,128)S(1)}, u32[]{:S(2)}, u32[]{:S(2)}) collective-permute-start(f32[16,16,128]{2,1,0:T(8,128)S(1)} %bitcast.80), channel_id=1, source_target_pairs={{0,16},{16,0},{1,17},{17,1},{2,18},{18,2},{3,19},{19,3},{4,20},{20... | collective-permute-start | bytes 393224 | tf_op jit(solution)/shard_map/ppermute | solution.py:270
  38.9 7.2 %collective-permute-start.18 = (f32[64,640]{1,0:T(8,128)S(1)}, f32[64,640]{1,0:T(8,128)S(1)}, u32[]{:S(2)}, u32[]{:S(2)}) collective-permute-start(f32[64,640]{1,0:T(8,128)S(1)} %get-tuple-element.130.own_ref), channel_id=1, source_target_pairs={{0,128},{128,0},{1,129},{129,1},{2,130},{130,2},{3,131},{131,3},{4... | collective-permute-start | bytes 491528 | tf_op jit(solution)/shard_map/ppermute | solution.py:270
  39.7 3.6 %collective-permute-start.17 = (f32[17,16,128]{2,1,0:T(8,128)S(1)}, f32[17,16,128]{2,1,0:T(8,128)S(1)}, u32[]{:S(2)}, u32[]{:S(2)}) collective-permute-start(f32[17,16,128]{2,1,0:T(8,128)S(1)} %get-tuple-element.163), channel_id=1, source_target_pairs={{0,16},{16,0},{1,17},{17,1},{2,18},{18,2},{3,19},{19,3},{4,20},{20... | collective-permute-start | bytes 417800 | tf_op jit(solution)/shard_map/ppermute | solution.py:270
  42.3 1.4 %collective-permute-start.16 = (f32[17,16,128]{2,1,0:T(8,128)S(1)}, f32[17,16,128]{2,1,0:T(8,128)S(1)}, u32[]{:S(2)}, u32[]{:S(2)}) collective-permute-start(f32[17,16,128]{2,1,0:T(8,128)S(1)} %get-tuple-element.164), channel_id=1, source_target_pairs={{0,16},{16,0},{1,17},{17,1},{2,18},{18,2},{3,19},{19,3},{4,20},{20... | collective-permute-start | bytes 417800 | tf_op jit(solution)/shard_map/ppermute | solution.py:270
  46.2 6.2 %collective-permute-start.19 = (f32[64,640]{1,0:T(8,128)S(1)}, f32[64,640]{1,0:T(8,128)S(1)}, u32[]{:S(2)}, u32[]{:S(2)}) collective-permute-start(f32[64,640]{1,0:T(8,128)S(1)} %shard_map.82.own_ref), channel_id=1, source_target_pairs={{0,128},{128,0},{1,129},{129,1},{2,130},{130,2},{3,131},{131,3},{4... | collective-permute-start | bytes 491528 | tf_op jit(solution)/shard_map/ppermute | solution.py:270
  49.2 5.0 %copy-start.2 = (f32[128,128]{1,0:T(8,128)S(1)}, f32[128,128]{1,0:T(8,128)}, u32[]{:S(2)}) copy-start(f32[128,128]{1,0:T(8,128)} %amp_ref.1) | copy-start | bytes 196612
  49.2 5.0 %copy-start.3 = (s32[2048]{0:T(1024)S(1)}, s32[2048]{0:T(1024)}, u32[]{:S(2)}) copy-start(s32[2048]{0:T(1024)} %param.13) | copy-start | bytes 24580
  49.2 5.0 %copy-start.4 = (f32[2048]{0:T(1024)S(1)}, f32[2048]{0:T(1024)}, u32[]{:S(2)}) copy-start(f32[2048]{0:T(1024)} %param.16) | copy-start | bytes 24580
  49.2 5.0 %copy-start.5 = (f32[640]{0:T(1024)S(1)}, f32[640]{0:T(1024)}, u32[]{:S(2)}) copy-start(f32[640]{0:T(1024)} %param.17) | copy-start | bytes 7684
  49.2 5.0 %copy-start.6 = (s32[128]{0:T(128)S(1)}, s32[128]{0:T(128)}, u32[]{:S(2)}) copy-start(s32[128]{0:T(128)} %param.14) | copy-start | bytes 1540
where the time goes:
time: 54.9 us; the launch traced here: 54.7 us
  starting transfers between devices  18.8 us (34%)
  Pallas kernels  12.2 us (22%)
  blocking collectives  11.1 us (20%)
  waiting for transfers between devices  11 us (20%)
  between operations  1.02 us (2%)
    ppermute x10, starting transfers between devices, swapped(): return lax.ppermute(x, axes, [(i, count - 1 - i) for i in range(count)])  18.8 us
    all_to_all x1, blocking collectives, one_pass(): met = lax.all_to_all(packed, NEAR, 0, 0, tiled=True)  11.1 us
    ppermute x10, waiting for transfers between devices, swapped(): return lax.ppermute(x, axes, [(i, count - 1 - i) for i in range(count)])  11 us
    pallas_call x2, Pallas kernels, expand(): pl.pallas_call(functools.partial(expand_kernel, side), out_shape=pltpu.HB...  3.63 us
    pallas_call x1, Pallas kernels, one_pass(): pl.pallas_call(load_kernel, out_shape=[shape((COLS, BLOCK, width), f32),...  2.59 us
    pallas_call x2, Pallas kernels, ladder(): pl.pallas_call(functools.partial(ladder_kernel, side), out_shape=[shape((...  2.06 us
    pallas_call x1, Pallas kernels, one_pass(): pl.pallas_call(table_kernel, out_shape=[shape((BLOCKS * HALF, width), f32...  1.47 us
    pallas_call x2, Pallas kernels, split(): pl.pallas_call(functools.partial(split_kernel, part), out_shape=[shape((d...  1.27 us
  transfers between devices with their start and end apart: 10, of which 8 were waited for; matrix products, arithmetic and copies ran while one was open for 0% of the time, Pallas kernels for 17%

commit v1 on v0

--- a/solution.py
+++ b/solution.py
@@ -94,8 +94,7 @@
     first = amp.astype(bf16)
     rest = amp - first.astype(f32)
     second = rest.astype(bf16)
-    third = (rest - second.astype(f32)).astype(bf16)
-    packed = mm(pick, first) + mm(pick, second) + mm(pick, third)
+    packed = mm(pick, first) + mm(pick, second)
     cd = cd_ref[...]
     sign = (1 - 2 * upper).astype(f32)
     tile = jnp.where(iota((META, BLOCK), 0) == number(COL[1:]), cd.astype(f32), 0.0)

time: 54.9 us -> 54.9 us (level)
  no operation moved by 1% of the time
where the time goes in v1:
time: 54.9 us; the launch traced here: 54.7 us
  starting transfers between devices  18.7 us (34%)
  Pallas kernels  12.2 us (22%)
  blocking collectives  11.1 us (20%)
  waiting for transfers between devices  11.1 us (20%)
  between operations  1.02 us (2%)
    ppermute x10, starting transfers between devices, swapped(): return lax.ppermute(x, axes, [(i, count - 1 - i) for i in range(count)])  18.7 us
    all_to_all x1, blocking collectives, one_pass(): met = lax.all_to_all(packed, NEAR, 0, 0, tiled=True)  11.1 us
    ppermute x10, waiting for transfers between devices, swapped(): return lax.ppermute(x, axes, [(i, count - 1 - i) for i in range(count)])  11.1 us
    pallas_call x2, Pallas kernels, expand(): pl.pallas_call(functools.partial(expand_kernel, side), out_shape=pltpu.HB...  3.63 us
    pallas_call x1, Pallas kernels, one_pass(): pl.pallas_call(load_kernel, out_shape=[shape((COLS, BLOCK, width), f32),...  2.59 us
    pallas_call x2, Pallas kernels, ladder(): pl.pallas_call(functools.partial(ladder_kernel, side), out_shape=[shape((...  2.08 us
    pallas_call x1, Pallas kernels, one_pass(): pl.pallas_call(table_kernel, out_shape=[shape((BLOCKS * HALF, width), f32...  1.47 us
    pallas_call x2, Pallas kernels, split(): pl.pallas_call(functools.partial(split_kernel, part), out_shape=[shape((d...  1.27 us
  transfers between devices with their start and end apart: 10, of which 8 were waited for; matrix products, arithmetic and copies ran while one was open for 0% of the time, Pallas kernels for 17%

profile of v1, /device:TPU:1, one launch (start us, length us, event | category | flops | bytes accessed | tf_op | source)
XLA Modules:
  0.0 54.7 jit_solution(14452868251469898555)
XLA Ops:
  0.0 0.0 copy-start.1
  0.0 1.2 %shard_map.76 = f32[8,24,128]{2,1,0:T(8,128)S(1)} custom-call(s32[1]{0:T(128)} %constant.2.clone.1.base_ref, f32[128,128]{1,0:T(8,128)} %amp_ref.1, s32[16,128]{1,0:T(8,128)} %bitcast.77, s32[1,128]{1,0:T(1,128)} %bitcast.86), custom_call_target="tpu_custom_call" | custom-call | tf_op jit(solution)/shard_map/pallas_call | solution.py:283
  1.2 11.1 %all_to_all.11 = f32[8,24,128]{2,1,0:T(8,128)S(1)} all-to-all(f32[8,24,128]{2,1,0:T(8,128)S(1)} %shard_map.76), channel_id=1, replica_groups=mesh['yh'=2,'yl'=2,'xh'=2,'core'=2,'xl'=2,'z2'=2,'z1'=2,'z0'=2] {'yh','y..., dimensions={0} | all-to-all | bytes 196608 | tf_op jit(solution)/shard_map/all_to_all | solution.py:314
  12.4 6.1 %collective-permute-start.10 = (f32[80,128]{1,0:T(8,128)S(1)}, f32[80,128]{1,0:T(8,128)S(1)}, u32[]{:S(2)}, u32[]{:S(2)}) collective-permute-start(f32[80,128]{1,0:T(8,128)S(1)} %pad_maximum_fusion.15), channel_id=1, source_target_pairs={{0,6},{2,4},{4,2},{6,0},{1,7},{3,5},{5,3},{7,1},{8,14},{10,12},{12... | collective-permute-start | bytes 122888 | tf_op jit(solution)/shard_map/ppermute | solution.py:269
  18.5 1.5 %shard_map.75 = (f32[128,640]{1,0:T(8,128)S(1)}, f32[128,128]{1,0:T(8,128)S(1)}, f32[1,16,128]{2,1,0:T(8,128)S(1)}, s32[1]{0:T(128)}) custom-call(s32[1]{0:T(128)} %constant.2.clone.1.base_ref, s32[16,128]{1,0:T(8,128)} %bitcast.78, f32[16,128]{1,0:T(8,128)} %bitcast.81, s32[5,128]{1,0:T(8,128)} %bitcast.65, f32[5,128]{1,0:T(8,128)} %bitcast.83), custom_call_target="tpu_custom_call" | custom-call | flops 1000 | bytes 1000 | tf_op jit(solution)/shard_map/pallas_call | solution.py:290
  20.0 0.0 collective-permute-done.10
  20.0 1.3 %collective-permute-start.11 = (f32[144,128]{1,0:T(8,128)S(1)}, f32[144,128]{1,0:T(8,128)S(1)}, u32[]{:S(2)}, u32[]{:S(2)}) collective-permute-start(f32[144,128]{1,0:T(8,128)S(1)} %pad_maximum_fusion.14), channel_id=1, source_target_pairs={{0,2},{2,0},{1,3},{3,1},{4,6},{6,4},{5,7},{7,5},{8,10},{10,8},{9,1... | collective-permute-start | bytes 221192 | tf_op jit(solution)/shard_map/ppermute | solution.py:269
  21.3 2.6 %shard_map.77 = (f32[16,128,640]{2,1,0:T(8,128)S(1)}, f32[1,16,128]{2,1,0:T(8,128)S(1)}) custom-call(f32[2048,640]{1,0:T(8,128)} %v_ref.1), custom_call_target="tpu_custom_call" | custom-call | flops 1000 | bytes 1000 | tf_op jit(solution)/shard_map/pallas_call | solution.py:304
  23.9 1.1 %collective-permute-done.11 = f32[144,128]{1,0:T(8,128)S(1)} collective-permute-done((f32[144,128]{1,0:T(8,128)S(1)}, f32[144,128]{1,0:T(8,128)S(1)}, u32[]{:S(2)}, u32[]{:S(2)}) %collective-permute-start.11) | collective-permute-done | bytes 73760 | tf_op jit(solution)/shard_map/ppermute | solution.py:269
  25.0 0.1 collective-permute-start.12
  25.2 0.0 copy-done.1
  25.2 0.6 %shard_map.78 = (bf16[1024,640]{1,0:T(8,128)(2,1)S(1)}, bf16[1024,640]{1,0:T(8,128)(2,1)S(1)}, f32[1,16,128]{2,1,0:T(8,128)S(1)}) custom-call(f32[16,128]{1,0:T(8,128)S(1)} %get-tuple-element.156.meta_ref, s32[5,128]{1,0:T(8,128)S(1)} %bitcast.66, f32[16,128,640]{2,1,0:T(8,128)S(1)} %get-tuple-element.121.held_ref), custom_call_target="tpu_custom_call" | custom-call | flops 1000 | bytes 1000 | tf_op jit(solution)/shard_map/pallas_call | solution.py:319
  25.8 3.5 %collective-permute-done.12 = f32[272,128]{1,0:T(8,128)S(1)} collective-permute-done((f32[272,128]{1,0:T(8,128)S(1)}, f32[272,128]{1,0:T(8,128)S(1)}, u32[]{:S(2)}, u32[]{:S(2)}) %collective-permute-start.12) | collective-permute-done | bytes 139296 | tf_op jit(solution)/shard_map/ppermute | solution.py:269
  29.3 1.8 %collective-permute-start.13 = (f32[33,16,128]{2,1,0:T(8,128)S(1)}, f32[33,16,128]{2,1,0:T(8,128)S(1)}, u32[]{:S(2)}, u32[]{:S(2)}) collective-permute-start(f32[33,16,128]{2,1,0:T(8,128)S(1)} %pad_maximum_fusion.8), channel_id=1, source_target_pairs={{0,40},{8,32},{32,8},{40,0},{1,41},{9,33},{33,9},{41,1},{2,42},{10... | collective-permute-start | bytes 811016 | tf_op jit(solution)/shard_map/ppermute | solution.py:269
  31.1 5.4 %collective-permute-start.14 = (f32[16,16,128]{2,1,0:T(8,128)S(1)}, f32[16,16,128]{2,1,0:T(8,128)S(1)}, u32[]{:S(2)}, u32[]{:S(2)}) collective-permute-start(f32[16,16,128]{2,1,0:T(8,128)S(1)} %bitcast.85), channel_id=1, source_target_pairs={{0,16},{16,0},{1,17},{17,1},{2,18},{18,2},{3,19},{19,3},{4,20},{20... | collective-permute-start | bytes 393224 | tf_op jit(solution)/shard_map/ppermute | solution.py:269
  36.5 0.1 collective-permute-start.15
  36.6 0.6 %shard_map.79 = (bf16[1024,640]{1,0:T(8,128)(2,1)S(1)}, bf16[1024,640]{1,0:T(8,128)(2,1)S(1)}, f32[1,16,128]{2,1,0:T(8,128)S(1)}) custom-call(f32[16,128]{1,0:T(8,128)S(1)} %slice_add_fusion.6.meta_ref, s32[5,128]{1,0:T(8,128)S(1)} %bitcast.67, f32[16,128,640]{2,1,0:T(8,128)S(1)} %get-tuple-element.121.held_ref), custom_call_target="tpu_custom_call" | custom-call | flops 1000 | bytes 1000 | tf_op jit(solution)/shard_map/pallas_call | solution.py:319
  37.3 0.2 collective-permute-done.14.refs_0_
  37.5 0.4 collective-permute-done.15.refs_1_
  37.9 1.0 %shard_map.80 = (f32[64,640]{1,0:T(8,128)S(1)}, f32[1,16,128]{2,1,0:T(8,128)S(1)}) custom-call(f32[32,16,128]{2,1,0:T(8,128)S(1)} %bitcast.54, f32[16,16,128]{2,1,0:T(8,128)S(1)} %collective-permute-done.14.refs_0_, f32[16,16,128]{2,1,0:T(8,128)S(1)} %collective-permute-done.15.refs_1_, bf16[1024,640]{1,0:T(8,128)(2,1)S(1)} %get-tuple-element.123.refs_2_, ...), custom_call_target="tpu_custom_call" | custom-call | flops 1000 | bytes 1000 | tf_op jit(solution)/shard_map/pallas_call | solution.py:342
  38.9 0.7 %collective-permute-start.18 = (f32[64,640]{1,0:T(8,128)S(1)}, f32[64,640]{1,0:T(8,128)S(1)}, u32[]{:S(2)}, u32[]{:S(2)}) collective-permute-start(f32[64,640]{1,0:T(8,128)S(1)} %get-tuple-element.130.own_ref), channel_id=1, source_target_pairs={{0,128},{128,0},{1,129},{129,1},{2,130},{130,2},{3,131},{131,3},{4... | collective-permute-start | bytes 491528 | tf_op jit(solution)/shard_map/ppermute | solution.py:269
  39.6 0.0 collective-permute-done.13
  39.7 2.6 %collective-permute-start.17 = (f32[17,16,128]{2,1,0:T(8,128)S(1)}, f32[17,16,128]{2,1,0:T(8,128)S(1)}, u32[]{:S(2)}, u32[]{:S(2)}) collective-permute-start(f32[17,16,128]{2,1,0:T(8,128)S(1)} %get-tuple-element.163), channel_id=1, source_target_pairs={{0,16},{16,0},{1,17},{17,1},{2,18},{18,2},{3,19},{19,3},{4,20},{20... | collective-permute-start | bytes 417800 | tf_op jit(solution)/shard_map/ppermute | solution.py:269
  42.3 0.1 collective-permute-start.16
  42.4 0.9 %collective-permute-done.17.refs_1_ = f32[17,16,128]{2,1,0:T(8,128)S(1)} collective-permute-done((f32[17,16,128]{2,1,0:T(8,128)S(1)}, f32[17,16,128]{2,1,0:T(8,128)S(1)}, u32[]{:S(2)}, u32[]{:S(2)}) %collective-permute-start.17) | collective-permute-done | bytes 139296 | tf_op jit(solution)/shard_map/ppermute | solution.py:269
  43.3 0.4 collective-permute-done.16.refs_0_
  43.6 1.0 %shard_map.81.in_ref = f32[64,640]{1,0:T(8,128)S(1)} custom-call(f32[32,16,128]{2,1,0:T(8,128)S(1)} %slice.116.near_ref, f32[17,16,128]{2,1,0:T(8,128)S(1)} %collective-permute-done.16.refs_0_, f32[17,16,128]{2,1,0:T(8,128)S(1)} %collective-permute-done.17.refs_1_, bf16[1024,640]{1,0:T(8,128)(2,1)S(1)} %get-tuple-element.123.refs_2_, ...), custom_call_target="tpu_custom_call" | custom-call | flops 1000 | bytes 1000 | tf_op jit(solution)/shard_map/pallas_call | solution.py:342
  44.7 1.5 %collective-permute-done.18.after_ref.other_ref = f32[64,640]{1,0:T(8,128)S(1)} collective-permute-done((f32[64,640]{1,0:T(8,128)S(1)}, f32[64,640]{1,0:T(8,128)S(1)}, u32[]{:S(2)}, u32[]{:S(2)}) %collective-permute-start.18) | collective-permute-done | bytes 163872 | tf_op jit(solution)/shard_map/ppermute | solution.py:269
  46.2 0.6 %collective-permute-start.19 = (f32[64,640]{1,0:T(8,128)S(1)}, f32[64,640]{1,0:T(8,128)S(1)}, u32[]{:S(2)}, u32[]{:S(2)}) collective-permute-start(f32[64,640]{1,0:T(8,128)S(1)} %shard_map.82.own_ref), channel_id=1, source_target_pairs={{0,128},{128,0},{1,129},{129,1},{2,130},{130,2},{3,131},{131,3},{4... | collective-permute-start | bytes 491528 | tf_op jit(solution)/shard_map/ppermute | solution.py:269
  47.3 1.8 %shard_map.83.refs_0_ = f32[2,8,128,640]{3,2,1,0:T(8,128)} custom-call(f32[64,640]{1,0:T(8,128)S(1)} %get-tuple-element.130.own_ref, f32[64,640]{1,0:T(8,128)S(1)} %collective-permute-done.18.after_ref.other_ref, f32[128,128]{1,0:T(8,128)S(1)} %get-tuple-element.131.rows_ref, s32[5,128]{1,0:T(8,128)S(1)} %bitcast.68), custom_call_target="tpu_custom_call" | custom-call | flops 1000 | bytes 1000 | tf_op jit(solution)/shard_map/pallas_call | solution.py:352
  49.1 0.0 copy-start.2
  49.1 0.0 copy-start.3
  49.2 0.0 copy-start.4
  49.2 0.0 copy-start.5
  49.2 0.0 copy-start.6
  49.2 3.2 %collective-permute-done.19.other_ref = f32[64,640]{1,0:T(8,128)S(1)} collective-permute-done((f32[64,640]{1,0:T(8,128)S(1)}, f32[64,640]{1,0:T(8,128)S(1)}, u32[]{:S(2)}, u32[]{:S(2)}) %collective-permute-start.19) | collective-permute-done | bytes 163872 | tf_op jit(solution)/shard_map/ppermute | solution.py:269
  52.4 1.8 %shard_map.84 = f32[2,8,128,640]{3,2,1,0:T(8,128)} custom-call(f32[64,640]{1,0:T(8,128)S(1)} %shard_map.82.own_ref, f32[64,640]{1,0:T(8,128)S(1)} %collective-permute-done.19.other_ref, f32[128,128]{1,0:T(8,128)S(1)} %get-tuple-element.131.rows_ref, s32[5,128]{1,0:T(8,128)S(1)} %bitcast.69, ...), custom_call_target="tpu_custom_call", output_to_operand_aliasing={{}: (4, {})} | custom-call | flops 1000 | bytes 1000 | tf_op jit(solution)/shard_map/pallas_call | solution.py:352
  54.2 0.0 copy-done.2
  54.2 0.0 copy-done.3
  54.2 0.0 copy-done.4
  54.3 0.0 copy-done.5
  54.3 0.0 copy-done.6
  54.3 0.2 conditional.1
  (20 shorter events, 0.2 us)
Async XLA Ops:
  0.0 25.2 %copy-start.1 = (s32[640]{0:T(1024)S(1)}, s32[640]{0:T(1024)}, u32[]{:S(2)}) copy-start(s32[640]{0:T(1024)} %param.15) | copy-start | bytes 7684
  12.4 7.6 %collective-permute-start.10 = (f32[80,128]{1,0:T(8,128)S(1)}, f32[80,128]{1,0:T(8,128)S(1)}, u32[]{:S(2)}, u32[]{:S(2)}) collective-permute-start(f32[80,128]{1,0:T(8,128)S(1)} %pad_maximum_fusion.15), channel_id=1, source_target_pairs={{0,6},{2,4},{4,2},{6,0},{1,7},{3,5},{5,3},{7,1},{8,14},{10,12},{12... | collective-permute-start | bytes 122888 | tf_op jit(solution)/shard_map/ppermute | solution.py:269
  20.0 5.0 %collective-permute-start.11 = (f32[144,128]{1,0:T(8,128)S(1)}, f32[144,128]{1,0:T(8,128)S(1)}, u32[]{:S(2)}, u32[]{:S(2)}) collective-permute-start(f32[144,128]{1,0:T(8,128)S(1)} %pad_maximum_fusion.14), channel_id=1, source_target_pairs={{0,2},{2,0},{1,3},{3,1},{4,6},{6,4},{5,7},{7,5},{8,10},{10,8},{9,1... | collective-permute-start | bytes 221192 | tf_op jit(solution)/shard_map/ppermute | solution.py:269
  25.0 4.2 %collective-permute-start.12 = (f32[272,128]{1,0:T(8,128)S(1)}, f32[272,128]{1,0:T(8,128)S(1)}, u32[]{:S(2)}, u32[]{:S(2)}) collective-permute-start(f32[272,128]{1,0:T(8,128)S(1)} %pad_maximum_fusion.12), channel_id=1, source_target_pairs={{0,1},{1,0},{2,3},{3,2},{4,5},{5,4},{6,7},{7,6},{8,9},{9,8},{10,11... | collective-permute-start | bytes 417800 | tf_op jit(solution)/shard_map/ppermute | solution.py:269
  29.3 10.3 %collective-permute-start.13 = (f32[33,16,128]{2,1,0:T(8,128)S(1)}, f32[33,16,128]{2,1,0:T(8,128)S(1)}, u32[]{:S(2)}, u32[]{:S(2)}) collective-permute-start(f32[33,16,128]{2,1,0:T(8,128)S(1)} %pad_maximum_fusion.8), channel_id=1, source_target_pairs={{0,40},{8,32},{32,8},{40,0},{1,41},{9,33},{33,9},{41,1},{2,42},{10... | collective-permute-start | bytes 811016 | tf_op jit(solution)/shard_map/ppermute | solution.py:269
  31.1 6.4 %collective-permute-start.14 = (f32[16,16,128]{2,1,0:T(8,128)S(1)}, f32[16,16,128]{2,1,0:T(8,128)S(1)}, u32[]{:S(2)}, u32[]{:S(2)}) collective-permute-start(f32[16,16,128]{2,1,0:T(8,128)S(1)} %bitcast.85), channel_id=1, source_target_pairs={{0,16},{16,0},{1,17},{17,1},{2,18},{18,2},{3,19},{19,3},{4,20},{20... | collective-permute-start | bytes 393224 | tf_op jit(solution)/shard_map/ppermute | solution.py:269
  36.5 1.3 %collective-permute-start.15 = (f32[16,16,128]{2,1,0:T(8,128)S(1)}, f32[16,16,128]{2,1,0:T(8,128)S(1)}, u32[]{:S(2)}, u32[]{:S(2)}) collective-permute-start(f32[16,16,128]{2,1,0:T(8,128)S(1)} %bitcast.80), channel_id=1, source_target_pairs={{0,16},{16,0},{1,17},{17,1},{2,18},{18,2},{3,19},{19,3},{4,20},{20... | collective-permute-start | bytes 393224 | tf_op jit(solution)/shard_map/ppermute | solution.py:269
  38.9 7.2 %collective-permute-start.18 = (f32[64,640]{1,0:T(8,128)S(1)}, f32[64,640]{1,0:T(8,128)S(1)}, u32[]{:S(2)}, u32[]{:S(2)}) collective-permute-start(f32[64,640]{1,0:T(8,128)S(1)} %get-tuple-element.130.own_ref), channel_id=1, source_target_pairs={{0,128},{128,0},{1,129},{129,1},{2,130},{130,2},{3,131},{131,3},{4... | collective-permute-start | bytes 491528 | tf_op jit(solution)/shard_map/ppermute | solution.py:269
  39.7 3.6 %collective-permute-start.17 = (f32[17,16,128]{2,1,0:T(8,128)S(1)}, f32[17,16,128]{2,1,0:T(8,128)S(1)}, u32[]{:S(2)}, u32[]{:S(2)}) collective-permute-start(f32[17,16,128]{2,1,0:T(8,128)S(1)} %get-tuple-element.163), channel_id=1, source_target_pairs={{0,16},{16,0},{1,17},{17,1},{2,18},{18,2},{3,19},{19,3},{4,20},{20... | collective-permute-start | bytes 417800 | tf_op jit(solution)/shard_map/ppermute | solution.py:269
  42.3 1.4 %collective-permute-start.16 = (f32[17,16,128]{2,1,0:T(8,128)S(1)}, f32[17,16,128]{2,1,0:T(8,128)S(1)}, u32[]{:S(2)}, u32[]{:S(2)}) collective-permute-start(f32[17,16,128]{2,1,0:T(8,128)S(1)} %get-tuple-element.164), channel_id=1, source_target_pairs={{0,16},{16,0},{1,17},{17,1},{2,18},{18,2},{3,19},{19,3},{4,20},{20... | collective-permute-start | bytes 417800 | tf_op jit(solution)/shard_map/ppermute | solution.py:269
  46.2 6.2 %collective-permute-start.19 = (f32[64,640]{1,0:T(8,128)S(1)}, f32[64,640]{1,0:T(8,128)S(1)}, u32[]{:S(2)}, u32[]{:S(2)}) collective-permute-start(f32[64,640]{1,0:T(8,128)S(1)} %shard_map.82.own_ref), channel_id=1, source_target_pairs={{0,128},{128,0},{1,129},{129,1},{2,130},{130,2},{3,131},{131,3},{4... | collective-permute-start | bytes 491528 | tf_op jit(solution)/shard_map/ppermute | solution.py:269
  49.1 5.1 %copy-start.2 = (f32[128,128]{1,0:T(8,128)S(1)}, f32[128,128]{1,0:T(8,128)}, u32[]{:S(2)}) copy-start(f32[128,128]{1,0:T(8,128)} %amp_ref.1) | copy-start | bytes 196612
  49.1 5.1 %copy-start.3 = (s32[2048]{0:T(1024)S(1)}, s32[2048]{0:T(1024)}, u32[]{:S(2)}) copy-start(s32[2048]{0:T(1024)} %param.13) | copy-start | bytes 24580
  49.2 5.1 %copy-start.4 = (f32[2048]{0:T(1024)S(1)}, f32[2048]{0:T(1024)}, u32[]{:S(2)}) copy-start(f32[2048]{0:T(1024)} %param.16) | copy-start | bytes 24580
  49.2 5.1 %copy-start.5 = (f32[640]{0:T(1024)S(1)}, f32[640]{0:T(1024)}, u32[]{:S(2)}) copy-start(f32[640]{0:T(1024)} %param.17) | copy-start | bytes 7684
  49.2 5.1 %copy-start.6 = (s32[128]{0:T(128)S(1)}, s32[128]{0:T(128)}, u32[]{:S(2)}) copy-start(s32[128]{0:T(128)} %param.14) | copy-start | bytes 1540

commit v2 on v1

--- a/solution.py
+++ b/solution.py
@@ -197,7 +197,7 @@
         ref[...] = jnp.zeros(ref.shape, f32)
     lines = PART * HALF
     total = None
-    group = 4
+    group = 8
     for j0 in range(0, COLS, group):
         left = [
             jnp.concatenate(

time: 54.9 us -> 54.9 us (level)
  no operation moved by 1% of the time
where the time goes in v2:
time: 54.9 us; the launch traced here: 54.7 us
  starting transfers between devices  18.8 us (34%)
  Pallas kernels  12.2 us (22%)
  blocking collectives  11.1 us (20%)
  waiting for transfers between devices  11.1 us (20%)
  between operations  1.02 us (2%)
    ppermute x10, starting transfers between devices, swapped(): return lax.ppermute(x, axes, [(i, count - 1 - i) for i in range(count)])  18.8 us
    all_to_all x1, blocking collectives, one_pass(): met = lax.all_to_all(packed, NEAR, 0, 0, tiled=True)  11.1 us
    ppermute x10, waiting for transfers between devices, swapped(): return lax.ppermute(x, axes, [(i, count - 1 - i) for i in range(count)])  11.1 us
    pallas_call x2, Pallas kernels, expand(): pl.pallas_call(functools.partial(expand_kernel, side), out_shape=pltpu.HB...  3.63 us
    pallas_call x1, Pallas kernels, one_pass(): pl.pallas_call(load_kernel, out_shape=[shape((COLS, BLOCK, width), f32),...  2.59 us
    pallas_call x2, Pallas kernels, ladder(): pl.pallas_call(functools.partial(ladder_kernel, side), out_shape=[shape((...  2.06 us
    pallas_call x1, Pallas kernels, one_pass(): pl.pallas_call(table_kernel, out_shape=[shape((BLOCKS * HALF, width), f32...  1.47 us
    pallas_call x2, Pallas kernels, split(): pl.pallas_call(functools.partial(split_kernel, part), out_shape=[shape((d...  1.27 us
  transfers between devices with their start and end apart: 10, of which 8 were waited for; matrix products, arithmetic and copies ran while one was open for 0% of the time, Pallas kernels for 17%

profile of v2, /device:TPU:1, one launch (start us, length us, event | category | flops | bytes accessed | tf_op | source)
XLA Modules:
  0.0 54.7 jit_solution(2458159120648635427)
XLA Ops:
  0.0 0.0 copy-start.1
  0.0 1.2 %shard_map.76 = f32[8,24,128]{2,1,0:T(8,128)S(1)} custom-call(s32[1]{0:T(128)} %constant.2.clone.1.base_ref, f32[128,128]{1,0:T(8,128)} %amp_ref.1, s32[16,128]{1,0:T(8,128)} %bitcast.77, s32[1,128]{1,0:T(1,128)} %bitcast.86), custom_call_target="tpu_custom_call" | custom-call | tf_op jit(solution)/shard_map/pallas_call | solution.py:283
  1.2 11.1 %all_to_all.11 = f32[8,24,128]{2,1,0:T(8,128)S(1)} all-to-all(f32[8,24,128]{2,1,0:T(8,128)S(1)} %shard_map.76), channel_id=1, replica_groups=mesh['yh'=2,'yl'=2,'xh'=2,'core'=2,'xl'=2,'z2'=2,'z1'=2,'z0'=2] {'yh','y..., dimensions={0} | all-to-all | bytes 196608 | tf_op jit(solution)/shard_map/all_to_all | solution.py:314
  12.4 6.1 %collective-permute-start.10 = (f32[80,128]{1,0:T(8,128)S(1)}, f32[80,128]{1,0:T(8,128)S(1)}, u32[]{:S(2)}, u32[]{:S(2)}) collective-permute-start(f32[80,128]{1,0:T(8,128)S(1)} %pad_maximum_fusion.15), channel_id=1, source_target_pairs={{0,6},{2,4},{4,2},{6,0},{1,7},{3,5},{5,3},{7,1},{8,14},{10,12},{12... | collective-permute-start | bytes 122888 | tf_op jit(solution)/shard_map/ppermute | solution.py:269
  18.5 1.5 %shard_map.75 = (f32[128,640]{1,0:T(8,128)S(1)}, f32[128,128]{1,0:T(8,128)S(1)}, f32[1,16,128]{2,1,0:T(8,128)S(1)}, s32[1]{0:T(128)}) custom-call(s32[1]{0:T(128)} %constant.2.clone.1.base_ref, s32[16,128]{1,0:T(8,128)} %bitcast.78, f32[16,128]{1,0:T(8,128)} %bitcast.81, s32[5,128]{1,0:T(8,128)} %bitcast.65, f32[5,128]{1,0:T(8,128)} %bitcast.83), custom_call_target="tpu_custom_call" | custom-call | flops 1000 | bytes 1000 | tf_op jit(solution)/shard_map/pallas_call | solution.py:290
  20.0 0.0 collective-permute-done.10
  20.0 1.3 %collective-permute-start.11 = (f32[144,128]{1,0:T(8,128)S(1)}, f32[144,128]{1,0:T(8,128)S(1)}, u32[]{:S(2)}, u32[]{:S(2)}) collective-permute-start(f32[144,128]{1,0:T(8,128)S(1)} %pad_maximum_fusion.14), channel_id=1, source_target_pairs={{0,2},{2,0},{1,3},{3,1},{4,6},{6,4},{5,7},{7,5},{8,10},{10,8},{9,1... | collective-permute-start | bytes 221192 | tf_op jit(solution)/shard_map/ppermute | solution.py:269
  21.3 2.6 %shard_map.77 = (f32[16,128,640]{2,1,0:T(8,128)S(1)}, f32[1,16,128]{2,1,0:T(8,128)S(1)}) custom-call(f32[2048,640]{1,0:T(8,128)} %v_ref.1), custom_call_target="tpu_custom_call" | custom-call | flops 1000 | bytes 1000 | tf_op jit(solution)/shard_map/pallas_call | solution.py:304
  23.9 1.1 %collective-permute-done.11 = f32[144,128]{1,0:T(8,128)S(1)} collective-permute-done((f32[144,128]{1,0:T(8,128)S(1)}, f32[144,128]{1,0:T(8,128)S(1)}, u32[]{:S(2)}, u32[]{:S(2)}) %collective-permute-start.11) | collective-permute-done | bytes 73760 | tf_op jit(solution)/shard_map/ppermute | solution.py:269
  25.0 0.1 collective-permute-start.12
  25.2 0.0 copy-done.1
  25.2 0.6 %shard_map.78 = (bf16[1024,640]{1,0:T(8,128)(2,1)S(1)}, bf16[1024,640]{1,0:T(8,128)(2,1)S(1)}, f32[1,16,128]{2,1,0:T(8,128)S(1)}) custom-call(f32[16,128]{1,0:T(8,128)S(1)} %get-tuple-element.156.meta_ref, s32[5,128]{1,0:T(8,128)S(1)} %bitcast.66, f32[16,128,640]{2,1,0:T(8,128)S(1)} %get-tuple-element.121.held_ref), custom_call_target="tpu_custom_call" | custom-call | flops 1000 | bytes 1000 | tf_op jit(solution)/shard_map/pallas_call | solution.py:319
  25.8 3.5 %collective-permute-done.12 = f32[272,128]{1,0:T(8,128)S(1)} collective-permute-done((f32[272,128]{1,0:T(8,128)S(1)}, f32[272,128]{1,0:T(8,128)S(1)}, u32[]{:S(2)}, u32[]{:S(2)}) %collective-permute-start.12) | collective-permute-done | bytes 139296 | tf_op jit(solution)/shard_map/ppermute | solution.py:269
  29.3 1.8 %collective-permute-start.13 = (f32[33,16,128]{2,1,0:T(8,128)S(1)}, f32[33,16,128]{2,1,0:T(8,128)S(1)}, u32[]{:S(2)}, u32[]{:S(2)}) collective-permute-start(f32[33,16,128]{2,1,0:T(8,128)S(1)} %pad_maximum_fusion.8), channel_id=1, source_target_pairs={{0,40},{8,32},{32,8},{40,0},{1,41},{9,33},{33,9},{41,1},{2,42},{10... | collective-permute-start | bytes 811016 | tf_op jit(solution)/shard_map/ppermute | solution.py:269
  31.1 5.4 %collective-permute-start.14 = (f32[16,16,128]{2,1,0:T(8,128)S(1)}, f32[16,16,128]{2,1,0:T(8,128)S(1)}, u32[]{:S(2)}, u32[]{:S(2)}) collective-permute-start(f32[16,16,128]{2,1,0:T(8,128)S(1)} %bitcast.85), channel_id=1, source_target_pairs={{0,16},{16,0},{1,17},{17,1},{2,18},{18,2},{3,19},{19,3},{4,20},{20... | collective-permute-start | bytes 393224 | tf_op jit(solution)/shard_map/ppermute | solution.py:269
  36.5 0.1 collective-permute-start.15
  36.6 0.6 %shard_map.79 = (bf16[1024,640]{1,0:T(8,128)(2,1)S(1)}, bf16[1024,640]{1,0:T(8,128)(2,1)S(1)}, f32[1,16,128]{2,1,0:T(8,128)S(1)}) custom-call(f32[16,128]{1,0:T(8,128)S(1)} %slice_add_fusion.6.meta_ref, s32[5,128]{1,0:T(8,128)S(1)} %bitcast.67, f32[16,128,640]{2,1,0:T(8,128)S(1)} %get-tuple-element.121.held_ref), custom_call_target="tpu_custom_call" | custom-call | flops 1000 | bytes 1000 | tf_op jit(solution)/shard_map/pallas_call | solution.py:319
  37.3 0.2 collective-permute-done.14.refs_0_
  37.5 0.4 collective-permute-done.15.refs_1_
  37.9 1.0 %shard_map.80 = (f32[64,640]{1,0:T(8,128)S(1)}, f32[1,16,128]{2,1,0:T(8,128)S(1)}) custom-call(f32[32,16,128]{2,1,0:T(8,128)S(1)} %bitcast.54, f32[16,16,128]{2,1,0:T(8,128)S(1)} %collective-permute-done.14.refs_0_, f32[16,16,128]{2,1,0:T(8,128)S(1)} %collective-permute-done.15.refs_1_, bf16[1024,640]{1,0:T(8,128)(2,1)S(1)} %get-tuple-element.123.refs_2_, ...), custom_call_target="tpu_custom_call" | custom-call | flops 1000 | bytes 1000 | tf_op jit(solution)/shard_map/pallas_call | solution.py:342
  38.9 0.7 %collective-permute-start.18 = (f32[64,640]{1,0:T(8,128)S(1)}, f32[64,640]{1,0:T(8,128)S(1)}, u32[]{:S(2)}, u32[]{:S(2)}) collective-permute-start(f32[64,640]{1,0:T(8,128)S(1)} %get-tuple-element.130.own_ref), channel_id=1, source_target_pairs={{0,128},{128,0},{1,129},{129,1},{2,130},{130,2},{3,131},{131,3},{4... | collective-permute-start | bytes 491528 | tf_op jit(solution)/shard_map/ppermute | solution.py:269
  39.6 0.0 collective-permute-done.13
  39.7 2.6 %collective-permute-start.17 = (f32[17,16,128]{2,1,0:T(8,128)S(1)}, f32[17,16,128]{2,1,0:T(8,128)S(1)}, u32[]{:S(2)}, u32[]{:S(2)}) collective-permute-start(f32[17,16,128]{2,1,0:T(8,128)S(1)} %get-tuple-element.163), channel_id=1, source_target_pairs={{0,16},{16,0},{1,17},{17,1},{2,18},{18,2},{3,19},{19,3},{4,20},{20... | collective-permute-start | bytes 417800 | tf_op jit(solution)/shard_map/ppermute | solution.py:269
  42.3 0.1 collective-permute-start.16
  42.4 0.9 %collective-permute-done.17.refs_1_ = f32[17,16,128]{2,1,0:T(8,128)S(1)} collective-permute-done((f32[17,16,128]{2,1,0:T(8,128)S(1)}, f32[17,16,128]{2,1,0:T(8,128)S(1)}, u32[]{:S(2)}, u32[]{:S(2)}) %collective-permute-start.17) | collective-permute-done | bytes 139296 | tf_op jit(solution)/shard_map/ppermute | solution.py:269
  43.3 0.4 collective-permute-done.16.refs_0_
  43.6 1.0 %shard_map.81.in_ref = f32[64,640]{1,0:T(8,128)S(1)} custom-call(f32[32,16,128]{2,1,0:T(8,128)S(1)} %slice.116.near_ref, f32[17,16,128]{2,1,0:T(8,128)S(1)} %collective-permute-done.16.refs_0_, f32[17,16,128]{2,1,0:T(8,128)S(1)} %collective-permute-done.17.refs_1_, bf16[1024,640]{1,0:T(8,128)(2,1)S(1)} %get-tuple-element.123.refs_2_, ...), custom_call_target="tpu_custom_call" | custom-call | flops 1000 | bytes 1000 | tf_op jit(solution)/shard_map/pallas_call | solution.py:342
  44.7 1.5 %collective-permute-done.18.after_ref.other_ref = f32[64,640]{1,0:T(8,128)S(1)} collective-permute-done((f32[64,640]{1,0:T(8,128)S(1)}, f32[64,640]{1,0:T(8,128)S(1)}, u32[]{:S(2)}, u32[]{:S(2)}) %collective-permute-start.18) | collective-permute-done | bytes 163872 | tf_op jit(solution)/shard_map/ppermute | solution.py:269
  46.1 0.6 %collective-permute-start.19 = (f32[64,640]{1,0:T(8,128)S(1)}, f32[64,640]{1,0:T(8,128)S(1)}, u32[]{:S(2)}, u32[]{:S(2)}) collective-permute-start(f32[64,640]{1,0:T(8,128)S(1)} %shard_map.82.own_ref), channel_id=1, source_target_pairs={{0,128},{128,0},{1,129},{129,1},{2,130},{130,2},{3,131},{131,3},{4... | collective-permute-start | bytes 491528 | tf_op jit(solution)/shard_map/ppermute | solution.py:269
  47.3 1.8 %shard_map.83.refs_0_ = f32[2,8,128,640]{3,2,1,0:T(8,128)} custom-call(f32[64,640]{1,0:T(8,128)S(1)} %get-tuple-element.130.own_ref, f32[64,640]{1,0:T(8,128)S(1)} %collective-permute-done.18.after_ref.other_ref, f32[128,128]{1,0:T(8,128)S(1)} %get-tuple-element.131.rows_ref, s32[5,128]{1,0:T(8,128)S(1)} %bitcast.68), custom_call_target="tpu_custom_call" | custom-call | flops 1000 | bytes 1000 | tf_op jit(solution)/shard_map/pallas_call | solution.py:352
  49.1 0.0 copy-start.2
  49.1 0.0 copy-start.3
  49.2 0.0 copy-start.4
  49.2 0.0 copy-start.5
  49.2 0.0 copy-start.6
  49.2 3.2 %collective-permute-done.19.other_ref = f32[64,640]{1,0:T(8,128)S(1)} collective-permute-done((f32[64,640]{1,0:T(8,128)S(1)}, f32[64,640]{1,0:T(8,128)S(1)}, u32[]{:S(2)}, u32[]{:S(2)}) %collective-permute-start.19) | collective-permute-done | bytes 163872 | tf_op jit(solution)/shard_map/ppermute | solution.py:269
  52.4 1.8 %shard_map.84 = f32[2,8,128,640]{3,2,1,0:T(8,128)} custom-call(f32[64,640]{1,0:T(8,128)S(1)} %shard_map.82.own_ref, f32[64,640]{1,0:T(8,128)S(1)} %collective-permute-done.19.other_ref, f32[128,128]{1,0:T(8,128)S(1)} %get-tuple-element.131.rows_ref, s32[5,128]{1,0:T(8,128)S(1)} %bitcast.69, ...), custom_call_target="tpu_custom_call", output_to_operand_aliasing={{}: (4, {})} | custom-call | flops 1000 | bytes 1000 | tf_op jit(solution)/shard_map/pallas_call | solution.py:352
  54.2 0.0 copy-done.2
  54.2 0.0 copy-done.3
  54.2 0.0 copy-done.4
  54.2 0.0 copy-done.5
  54.2 0.0 copy-done.6
  54.2 0.2 conditional.1
  (20 shorter events, 0.2 us)
Async XLA Ops:
  0.0 25.2 %copy-start.1 = (s32[640]{0:T(1024)S(1)}, s32[640]{0:T(1024)}, u32[]{:S(2)}) copy-start(s32[640]{0:T(1024)} %param.15) | copy-start | bytes 7684
  12.4 7.6 %collective-permute-start.10 = (f32[80,128]{1,0:T(8,128)S(1)}, f32[80,128]{1,0:T(8,128)S(1)}, u32[]{:S(2)}, u32[]{:S(2)}) collective-permute-start(f32[80,128]{1,0:T(8,128)S(1)} %pad_maximum_fusion.15), channel_id=1, source_target_pairs={{0,6},{2,4},{4,2},{6,0},{1,7},{3,5},{5,3},{7,1},{8,14},{10,12},{12... | collective-permute-start | bytes 122888 | tf_op jit(solution)/shard_map/ppermute | solution.py:269
  20.0 5.0 %collective-permute-start.11 = (f32[144,128]{1,0:T(8,128)S(1)}, f32[144,128]{1,0:T(8,128)S(1)}, u32[]{:S(2)}, u32[]{:S(2)}) collective-permute-start(f32[144,128]{1,0:T(8,128)S(1)} %pad_maximum_fusion.14), channel_id=1, source_target_pairs={{0,2},{2,0},{1,3},{3,1},{4,6},{6,4},{5,7},{7,5},{8,10},{10,8},{9,1... | collective-permute-start | bytes 221192 | tf_op jit(solution)/shard_map/ppermute | solution.py:269
  25.0 4.2 %collective-permute-start.12 = (f32[272,128]{1,0:T(8,128)S(1)}, f32[272,128]{1,0:T(8,128)S(1)}, u32[]{:S(2)}, u32[]{:S(2)}) collective-permute-start(f32[272,128]{1,0:T(8,128)S(1)} %pad_maximum_fusion.12), channel_id=1, source_target_pairs={{0,1},{1,0},{2,3},{3,2},{4,5},{5,4},{6,7},{7,6},{8,9},{9,8},{10,11... | collective-permute-start | bytes 417800 | tf_op jit(solution)/shard_map/ppermute | solution.py:269
  29.3 10.3 %collective-permute-start.13 = (f32[33,16,128]{2,1,0:T(8,128)S(1)}, f32[33,16,128]{2,1,0:T(8,128)S(1)}, u32[]{:S(2)}, u32[]{:S(2)}) collective-permute-start(f32[33,16,128]{2,1,0:T(8,128)S(1)} %pad_maximum_fusion.8), channel_id=1, source_target_pairs={{0,40},{8,32},{32,8},{40,0},{1,41},{9,33},{33,9},{41,1},{2,42},{10... | collective-permute-start | bytes 811016 | tf_op jit(solution)/shard_map/ppermute | solution.py:269
  31.1 6.4 %collective-permute-start.14 = (f32[16,16,128]{2,1,0:T(8,128)S(1)}, f32[16,16,128]{2,1,0:T(8,128)S(1)}, u32[]{:S(2)}, u32[]{:S(2)}) collective-permute-start(f32[16,16,128]{2,1,0:T(8,128)S(1)} %bitcast.85), channel_id=1, source_target_pairs={{0,16},{16,0},{1,17},{17,1},{2,18},{18,2},{3,19},{19,3},{4,20},{20... | collective-permute-start | bytes 393224 | tf_op jit(solution)/shard_map/ppermute | solution.py:269
  36.5 1.3 %collective-permute-start.15 = (f32[16,16,128]{2,1,0:T(8,128)S(1)}, f32[16,16,128]{2,1,0:T(8,128)S(1)}, u32[]{:S(2)}, u32[]{:S(2)}) collective-permute-start(f32[16,16,128]{2,1,0:T(8,128)S(1)} %bitcast.80), channel_id=1, source_target_pairs={{0,16},{16,0},{1,17},{17,1},{2,18},{18,2},{3,19},{19,3},{4,20},{20... | collective-permute-start | bytes 393224 | tf_op jit(solution)/shard_map/ppermute | solution.py:269
  38.9 7.2 %collective-permute-start.18 = (f32[64,640]{1,0:T(8,128)S(1)}, f32[64,640]{1,0:T(8,128)S(1)}, u32[]{:S(2)}, u32[]{:S(2)}) collective-permute-start(f32[64,640]{1,0:T(8,128)S(1)} %get-tuple-element.130.own_ref), channel_id=1, source_target_pairs={{0,128},{128,0},{1,129},{129,1},{2,130},{130,2},{3,131},{131,3},{4... | collective-permute-start | bytes 491528 | tf_op jit(solution)/shard_map/ppermute | solution.py:269
  39.7 3.6 %collective-permute-start.17 = (f32[17,16,128]{2,1,0:T(8,128)S(1)}, f32[17,16,128]{2,1,0:T(8,128)S(1)}, u32[]{:S(2)}, u32[]{:S(2)}) collective-permute-start(f32[17,16,128]{2,1,0:T(8,128)S(1)} %get-tuple-element.163), channel_id=1, source_target_pairs={{0,16},{16,0},{1,17},{17,1},{2,18},{18,2},{3,19},{19,3},{4,20},{20... | collective-permute-start | bytes 417800 | tf_op jit(solution)/shard_map/ppermute | solution.py:269
  42.3 1.4 %collective-permute-start.16 = (f32[17,16,128]{2,1,0:T(8,128)S(1)}, f32[17,16,128]{2,1,0:T(8,128)S(1)}, u32[]{:S(2)}, u32[]{:S(2)}) collective-permute-start(f32[17,16,128]{2,1,0:T(8,128)S(1)} %get-tuple-element.164), channel_id=1, source_target_pairs={{0,16},{16,0},{1,17},{17,1},{2,18},{18,2},{3,19},{19,3},{4,20},{20... | collective-permute-start | bytes 417800 | tf_op jit(solution)/shard_map/ppermute | solution.py:269
  46.1 6.2 %collective-permute-start.19 = (f32[64,640]{1,0:T(8,128)S(1)}, f32[64,640]{1,0:T(8,128)S(1)}, u32[]{:S(2)}, u32[]{:S(2)}) collective-permute-start(f32[64,640]{1,0:T(8,128)S(1)} %shard_map.82.own_ref), channel_id=1, source_target_pairs={{0,128},{128,0},{1,129},{129,1},{2,130},{130,2},{3,131},{131,3},{4... | collective-permute-start | bytes 491528 | tf_op jit(solution)/shard_map/ppermute | solution.py:269
  49.1 5.1 %copy-start.2 = (f32[128,128]{1,0:T(8,128)S(1)}, f32[128,128]{1,0:T(8,128)}, u32[]{:S(2)}) copy-start(f32[128,128]{1,0:T(8,128)} %amp_ref.1) | copy-start | bytes 196612
  49.1 5.1 %copy-start.3 = (s32[2048]{0:T(1024)S(1)}, s32[2048]{0:T(1024)}, u32[]{:S(2)}) copy-start(s32[2048]{0:T(1024)} %param.13) | copy-start | bytes 24580
  49.2 5.0 %copy-start.4 = (f32[2048]{0:T(1024)S(1)}, f32[2048]{0:T(1024)}, u32[]{:S(2)}) copy-start(f32[2048]{0:T(1024)} %param.16) | copy-start | bytes 24580
  49.2 5.0 %copy-start.5 = (f32[640]{0:T(1024)S(1)}, f32[640]{0:T(1024)}, u32[]{:S(2)}) copy-start(f32[640]{0:T(1024)} %param.17) | copy-start | bytes 7684
  49.2 5.0 %copy-start.6 = (s32[128]{0:T(128)S(1)}, s32[128]{0:T(128)}, u32[]{:S(2)}) copy-start(s32[128]{0:T(128)} %param.14) | copy-start | bytes 1540

commit v3 on v1

--- a/solution.py
+++ b/solution.py
@@ -23,7 +23,7 @@
 
 NEAR = ("yh", "yl", "xl")
 COL_STEPS = (("z2", "z1"), ("z1",), ("z0",))
-X_STEP = ("xh", "xl")
+X_STEP = ("xh",)
 
 f32, bf16, i32 = jnp.float32, jnp.bfloat16, jnp.int32
 MIB = 1 << 20

time: 54.9 us -> 55.6 us (1.013)
  starting transfers between devices: 18.7 us -> 19.4 us
    ppermute x10, starting transfers between devices: 18.7 us -> 19.4 us  [swapped(): return lax.ppermute(x, axes, [(i, count - 1 - i) for i in range(count)])]
where the time goes in v3:
time: 55.6 us; the launch traced here: 55.4 us
  starting transfers between devices  19.4 us (35%)
  Pallas kernels  12.2 us (22%)
  waiting for transfers between devices  11.2 us (20%)
  blocking collectives  11.1 us (20%)
  between operations  1.02 us (2%)
    ppermute x10, starting transfers between devices, swapped(): return lax.ppermute(x, axes, [(i, count - 1 - i) for i in range(count)])  19.4 us
    ppermute x10, waiting for transfers between devices, swapped(): return lax.ppermute(x, axes, [(i, count - 1 - i) for i in range(count)])  11.2 us
    all_to_all x1, blocking collectives, one_pass(): met = lax.all_to_all(packed, NEAR, 0, 0, tiled=True)  11.1 us
    pallas_call x2, Pallas kernels, expand(): pl.pallas_call(functools.partial(expand_kernel, side), out_shape=pltpu.HB...  3.63 us
    pallas_call x1, Pallas kernels, one_pass(): pl.pallas_call(load_kernel, out_shape=[shape((COLS, BLOCK, width), f32),...  2.59 us
    pallas_call x2, Pallas kernels, ladder(): pl.pallas_call(functools.partial(ladder_kernel, side), out_shape=[shape((...  2.05 us
    pallas_call x1, Pallas kernels, one_pass(): pl.pallas_call(table_kernel, out_shape=[shape((BLOCKS * HALF, width), f32...  1.47 us
    pallas_call x2, Pallas kernels, split(): pl.pallas_call(functools.partial(split_kernel, part), out_shape=[shape((d...  1.27 us
  transfers between devices with their start and end apart: 10, of which 8 were waited for; matrix products, arithmetic and copies ran while one was open for 0% of the time, Pallas kernels for 17%

profile of v3, /device:TPU:1, one launch (start us, length us, event | category | flops | bytes accessed | tf_op | source)
XLA Modules:
  0.0 55.4 jit_solution(9941912749787722100)
XLA Ops:
  0.0 0.0 copy-start.1
  0.0 1.2 %shard_map.76 = f32[8,24,128]{2,1,0:T(8,128)S(1)} custom-call(s32[1]{0:T(128)} %constant.2.clone.1.base_ref, f32[128,128]{1,0:T(8,128)} %amp_ref.1, s32[16,128]{1,0:T(8,128)} %bitcast.77, s32[1,128]{1,0:T(1,128)} %bitcast.86), custom_call_target="tpu_custom_call" | custom-call | tf_op jit(solution)/shard_map/pallas_call | solution.py:283
  1.2 11.1 %all_to_all.11 = f32[8,24,128]{2,1,0:T(8,128)S(1)} all-to-all(f32[8,24,128]{2,1,0:T(8,128)S(1)} %shard_map.76), channel_id=1, replica_groups=mesh['yh'=2,'yl'=2,'xh'=2,'core'=2,'xl'=2,'z2'=2,'z1'=2,'z0'=2] {'yh','y..., dimensions={0} | all-to-all | bytes 196608 | tf_op jit(solution)/shard_map/all_to_all | solution.py:314
  12.4 6.1 %collective-permute-start.10 = (f32[80,128]{1,0:T(8,128)S(1)}, f32[80,128]{1,0:T(8,128)S(1)}, u32[]{:S(2)}, u32[]{:S(2)}) collective-permute-start(f32[80,128]{1,0:T(8,128)S(1)} %pad_maximum_fusion.15), channel_id=1, source_target_pairs={{0,6},{2,4},{4,2},{6,0},{1,7},{3,5},{5,3},{7,1},{8,14},{10,12},{12... | collective-permute-start | bytes 122888 | tf_op jit(solution)/shard_map/ppermute | solution.py:269
  18.5 1.5 %shard_map.75 = (f32[128,640]{1,0:T(8,128)S(1)}, f32[128,128]{1,0:T(8,128)S(1)}, f32[1,16,128]{2,1,0:T(8,128)S(1)}, s32[1]{0:T(128)}) custom-call(s32[1]{0:T(128)} %constant.2.clone.1.base_ref, s32[16,128]{1,0:T(8,128)} %bitcast.78, f32[16,128]{1,0:T(8,128)} %bitcast.81, s32[5,128]{1,0:T(8,128)} %bitcast.65, f32[5,128]{1,0:T(8,128)} %bitcast.83), custom_call_target="tpu_custom_call" | custom-call | flops 1000 | bytes 1000 | tf_op jit(solution)/shard_map/pallas_call | solution.py:290
  20.0 0.0 collective-permute-done.10
  20.0 1.3 %collective-permute-start.11 = (f32[144,128]{1,0:T(8,128)S(1)}, f32[144,128]{1,0:T(8,128)S(1)}, u32[]{:S(2)}, u32[]{:S(2)}) collective-permute-start(f32[144,128]{1,0:T(8,128)S(1)} %pad_maximum_fusion.14), channel_id=1, source_target_pairs={{0,2},{2,0},{1,3},{3,1},{4,6},{6,4},{5,7},{7,5},{8,10},{10,8},{9,1... | collective-permute-start | bytes 221192 | tf_op jit(solution)/shard_map/ppermute | solution.py:269
  21.3 2.6 %shard_map.77 = (f32[16,128,640]{2,1,0:T(8,128)S(1)}, f32[1,16,128]{2,1,0:T(8,128)S(1)}) custom-call(f32[2048,640]{1,0:T(8,128)} %v_ref.1), custom_call_target="tpu_custom_call" | custom-call | flops 1000 | bytes 1000 | tf_op jit(solution)/shard_map/pallas_call | solution.py:304
  23.9 1.1 %collective-permute-done.11 = f32[144,128]{1,0:T(8,128)S(1)} collective-permute-done((f32[144,128]{1,0:T(8,128)S(1)}, f32[144,128]{1,0:T(8,128)S(1)}, u32[]{:S(2)}, u32[]{:S(2)}) %collective-permute-start.11) | collective-permute-done | bytes 73760 | tf_op jit(solution)/shard_map/ppermute | solution.py:269
  25.0 0.1 collective-permute-start.12
  25.2 0.0 copy-done.1
  25.2 0.6 %shard_map.78 = (bf16[1024,640]{1,0:T(8,128)(2,1)S(1)}, bf16[1024,640]{1,0:T(8,128)(2,1)S(1)}, f32[1,16,128]{2,1,0:T(8,128)S(1)}) custom-call(f32[16,128]{1,0:T(8,128)S(1)} %get-tuple-element.156.meta_ref, s32[5,128]{1,0:T(8,128)S(1)} %bitcast.66, f32[16,128,640]{2,1,0:T(8,128)S(1)} %get-tuple-element.121.held_ref), custom_call_target="tpu_custom_call" | custom-call | flops 1000 | bytes 1000 | tf_op jit(solution)/shard_map/pallas_call | solution.py:319
  25.8 3.5 %collective-permute-done.12 = f32[272,128]{1,0:T(8,128)S(1)} collective-permute-done((f32[272,128]{1,0:T(8,128)S(1)}, f32[272,128]{1,0:T(8,128)S(1)}, u32[]{:S(2)}, u32[]{:S(2)}) %collective-permute-start.12) | collective-permute-done | bytes 139296 | tf_op jit(solution)/shard_map/ppermute | solution.py:269
  29.3 2.5 %collective-permute-start.13 = (f32[33,16,128]{2,1,0:T(8,128)S(1)}, f32[33,16,128]{2,1,0:T(8,128)S(1)}, u32[]{:S(2)}, u32[]{:S(2)}) collective-permute-start(f32[33,16,128]{2,1,0:T(8,128)S(1)} %pad_maximum_fusion.8), channel_id=1, source_target_pairs={{0,32},{32,0},{1,33},{33,1},{2,34},{34,2},{3,35},{35,3},{4,36},{36... | collective-permute-start | bytes 811016 | tf_op jit(solution)/shard_map/ppermute | solution.py:269
  31.9 5.4 %collective-permute-start.14 = (f32[16,16,128]{2,1,0:T(8,128)S(1)}, f32[16,16,128]{2,1,0:T(8,128)S(1)}, u32[]{:S(2)}, u32[]{:S(2)}) collective-permute-start(f32[16,16,128]{2,1,0:T(8,128)S(1)} %bitcast.85), channel_id=1, source_target_pairs={{0,16},{16,0},{1,17},{17,1},{2,18},{18,2},{3,19},{19,3},{4,20},{20... | collective-permute-start | bytes 393224 | tf_op jit(solution)/shard_map/ppermute | solution.py:269
  37.3 0.1 collective-permute-start.15
  37.4 0.6 %shard_map.79 = (bf16[1024,640]{1,0:T(8,128)(2,1)S(1)}, bf16[1024,640]{1,0:T(8,128)(2,1)S(1)}, f32[1,16,128]{2,1,0:T(8,128)S(1)}) custom-call(f32[16,128]{1,0:T(8,128)S(1)} %slice_add_fusion.6.meta_ref, s32[5,128]{1,0:T(8,128)S(1)} %bitcast.67, f32[16,128,640]{2,1,0:T(8,128)S(1)} %get-tuple-element.121.held_ref), custom_call_target="tpu_custom_call" | custom-call | flops 1000 | bytes 1000 | tf_op jit(solution)/shard_map/pallas_call | solution.py:319
  38.0 0.2 collective-permute-done.14.refs_0_
  38.3 0.4 collective-permute-done.15.refs_1_
  38.6 1.0 %shard_map.80 = (f32[64,640]{1,0:T(8,128)S(1)}, f32[1,16,128]{2,1,0:T(8,128)S(1)}) custom-call(f32[32,16,128]{2,1,0:T(8,128)S(1)} %bitcast.54, f32[16,16,128]{2,1,0:T(8,128)S(1)} %collective-permute-done.14.refs_0_, f32[16,16,128]{2,1,0:T(8,128)S(1)} %collective-permute-done.15.refs_1_, bf16[1024,640]{1,0:T(8,128)(2,1)S(1)} %get-tuple-element.123.refs_2_, ...), custom_call_target="tpu_custom_call" | custom-call | flops 1000 | bytes 1000 | tf_op jit(solution)/shard_map/pallas_call | solution.py:342
  39.7 1.0 %collective-permute-start.18 = (f32[64,640]{1,0:T(8,128)S(1)}, f32[64,640]{1,0:T(8,128)S(1)}, u32[]{:S(2)}, u32[]{:S(2)}) collective-permute-start(f32[64,640]{1,0:T(8,128)S(1)} %get-tuple-element.130.own_ref), channel_id=1, source_target_pairs={{0,128},{128,0},{1,129},{129,1},{2,130},{130,2},{3,131},{131,3},{4... | collective-permute-start | bytes 491528 | tf_op jit(solution)/shard_map/ppermute | solution.py:269
  40.7 0.0 collective-permute-done.13
  40.7 1.8 %collective-permute-start.17 = (f32[17,16,128]{2,1,0:T(8,128)S(1)}, f32[17,16,128]{2,1,0:T(8,128)S(1)}, u32[]{:S(2)}, u32[]{:S(2)}) collective-permute-start(f32[17,16,128]{2,1,0:T(8,128)S(1)} %get-tuple-element.163), channel_id=1, source_target_pairs={{0,16},{16,0},{1,17},{17,1},{2,18},{18,2},{3,19},{19,3},{4,20},{20... | collective-permute-start | bytes 417800 | tf_op jit(solution)/shard_map/ppermute | solution.py:269
  42.5 0.1 collective-permute-start.16
  42.7 0.9 %collective-permute-done.17.refs_1_ = f32[17,16,128]{2,1,0:T(8,128)S(1)} collective-permute-done((f32[17,16,128]{2,1,0:T(8,128)S(1)}, f32[17,16,128]{2,1,0:T(8,128)S(1)}, u32[]{:S(2)}, u32[]{:S(2)}) %collective-permute-start.17) | collective-permute-done | bytes 139296 | tf_op jit(solution)/shard_map/ppermute | solution.py:269
  43.5 0.4 collective-permute-done.16.refs_0_
  43.9 1.0 %shard_map.81.in_ref = f32[64,640]{1,0:T(8,128)S(1)} custom-call(f32[32,16,128]{2,1,0:T(8,128)S(1)} %slice.116.near_ref, f32[17,16,128]{2,1,0:T(8,128)S(1)} %collective-permute-done.16.refs_0_, f32[17,16,128]{2,1,0:T(8,128)S(1)} %collective-permute-done.17.refs_1_, bf16[1024,640]{1,0:T(8,128)(2,1)S(1)} %get-tuple-element.123.refs_2_, ...), custom_call_target="tpu_custom_call" | custom-call | flops 1000 | bytes 1000 | tf_op jit(solution)/shard_map/pallas_call | solution.py:342
  44.9 1.9 %collective-permute-done.18.after_ref.other_ref = f32[64,640]{1,0:T(8,128)S(1)} collective-permute-done((f32[64,640]{1,0:T(8,128)S(1)}, f32[64,640]{1,0:T(8,128)S(1)}, u32[]{:S(2)}, u32[]{:S(2)}) %collective-permute-start.18) | collective-permute-done | bytes 163872 | tf_op jit(solution)/shard_map/ppermute | solution.py:269
  46.9 0.9 %collective-permute-start.19 = (f32[64,640]{1,0:T(8,128)S(1)}, f32[64,640]{1,0:T(8,128)S(1)}, u32[]{:S(2)}, u32[]{:S(2)}) collective-permute-start(f32[64,640]{1,0:T(8,128)S(1)} %shard_map.82.own_ref), channel_id=1, source_target_pairs={{0,128},{128,0},{1,129},{129,1},{2,130},{130,2},{3,131},{131,3},{4... | collective-permute-start | bytes 491528 | tf_op jit(solution)/shard_map/ppermute | solution.py:269
  48.4 1.8 %shard_map.83.refs_0_ = f32[2,8,128,640]{3,2,1,0:T(8,128)} custom-call(f32[64,640]{1,0:T(8,128)S(1)} %get-tuple-element.130.own_ref, f32[64,640]{1,0:T(8,128)S(1)} %collective-permute-done.18.after_ref.other_ref, f32[128,128]{1,0:T(8,128)S(1)} %get-tuple-element.131.rows_ref, s32[5,128]{1,0:T(8,128)S(1)} %bitcast.68), custom_call_target="tpu_custom_call" | custom-call | flops 1000 | bytes 1000 | tf_op jit(solution)/shard_map/pallas_call | solution.py:352
  50.2 0.0 copy-start.2
  50.2 0.0 copy-start.3
  50.2 0.0 copy-start.4
  50.2 0.0 copy-start.5
  50.2 0.0 copy-start.6
  50.3 2.8 %collective-permute-done.19.other_ref = f32[64,640]{1,0:T(8,128)S(1)} collective-permute-done((f32[64,640]{1,0:T(8,128)S(1)}, f32[64,640]{1,0:T(8,128)S(1)}, u32[]{:S(2)}, u32[]{:S(2)}) %collective-permute-start.19) | collective-permute-done | bytes 163872 | tf_op jit(solution)/shard_map/ppermute | solution.py:269
  53.1 1.8 %shard_map.84 = f32[2,8,128,640]{3,2,1,0:T(8,128)} custom-call(f32[64,640]{1,0:T(8,128)S(1)} %shard_map.82.own_ref, f32[64,640]{1,0:T(8,128)S(1)} %collective-permute-done.19.other_ref, f32[128,128]{1,0:T(8,128)S(1)} %get-tuple-element.131.rows_ref, s32[5,128]{1,0:T(8,128)S(1)} %bitcast.69, ...), custom_call_target="tpu_custom_call", output_to_operand_aliasing={{}: (4, {})} | custom-call | flops 1000 | bytes 1000 | tf_op jit(solution)/shard_map/pallas_call | solution.py:352
  54.9 0.0 copy-done.2
  54.9 0.0 copy-done.3
  54.9 0.0 copy-done.4
  54.9 0.0 copy-done.5
  54.9 0.0 copy-done.6
  55.0 0.2 conditional.1
  (20 shorter events, 0.2 us)
Async XLA Ops:
  0.0 25.2 %copy-start.1 = (s32[640]{0:T(1024)S(1)}, s32[640]{0:T(1024)}, u32[]{:S(2)}) copy-start(s32[640]{0:T(1024)} %param.15) | copy-start | bytes 7684
  12.4 7.6 %collective-permute-start.10 = (f32[80,128]{1,0:T(8,128)S(1)}, f32[80,128]{1,0:T(8,128)S(1)}, u32[]{:S(2)}, u32[]{:S(2)}) collective-permute-start(f32[80,128]{1,0:T(8,128)S(1)} %pad_maximum_fusion.15), channel_id=1, source_target_pairs={{0,6},{2,4},{4,2},{6,0},{1,7},{3,5},{5,3},{7,1},{8,14},{10,12},{12... | collective-permute-start | bytes 122888 | tf_op jit(solution)/shard_map/ppermute | solution.py:269
  20.0 5.0 %collective-permute-start.11 = (f32[144,128]{1,0:T(8,128)S(1)}, f32[144,128]{1,0:T(8,128)S(1)}, u32[]{:S(2)}, u32[]{:S(2)}) collective-permute-start(f32[144,128]{1,0:T(8,128)S(1)} %pad_maximum_fusion.14), channel_id=1, source_target_pairs={{0,2},{2,0},{1,3},{3,1},{4,6},{6,4},{5,7},{7,5},{8,10},{10,8},{9,1... | collective-permute-start | bytes 221192 | tf_op jit(solution)/shard_map/ppermute | solution.py:269
  25.0 4.2 %collective-permute-start.12 = (f32[272,128]{1,0:T(8,128)S(1)}, f32[272,128]{1,0:T(8,128)S(1)}, u32[]{:S(2)}, u32[]{:S(2)}) collective-permute-start(f32[272,128]{1,0:T(8,128)S(1)} %pad_maximum_fusion.12), channel_id=1, source_target_pairs={{0,1},{1,0},{2,3},{3,2},{4,5},{5,4},{6,7},{7,6},{8,9},{9,8},{10,11... | collective-permute-start | bytes 417800 | tf_op jit(solution)/shard_map/ppermute | solution.py:269
  29.3 11.3 %collective-permute-start.13 = (f32[33,16,128]{2,1,0:T(8,128)S(1)}, f32[33,16,128]{2,1,0:T(8,128)S(1)}, u32[]{:S(2)}, u32[]{:S(2)}) collective-permute-start(f32[33,16,128]{2,1,0:T(8,128)S(1)} %pad_maximum_fusion.8), channel_id=1, source_target_pairs={{0,32},{32,0},{1,33},{33,1},{2,34},{34,2},{3,35},{35,3},{4,36},{36... | collective-permute-start | bytes 811016 | tf_op jit(solution)/shard_map/ppermute | solution.py:269
  31.9 6.4 %collective-permute-start.14 = (f32[16,16,128]{2,1,0:T(8,128)S(1)}, f32[16,16,128]{2,1,0:T(8,128)S(1)}, u32[]{:S(2)}, u32[]{:S(2)}) collective-permute-start(f32[16,16,128]{2,1,0:T(8,128)S(1)} %bitcast.85), channel_id=1, source_target_pairs={{0,16},{16,0},{1,17},{17,1},{2,18},{18,2},{3,19},{19,3},{4,20},{20... | collective-permute-start | bytes 393224 | tf_op jit(solution)/shard_map/ppermute | solution.py:269
  37.3 1.3 %collective-permute-start.15 = (f32[16,16,128]{2,1,0:T(8,128)S(1)}, f32[16,16,128]{2,1,0:T(8,128)S(1)}, u32[]{:S(2)}, u32[]{:S(2)}) collective-permute-start(f32[16,16,128]{2,1,0:T(8,128)S(1)} %bitcast.80), channel_id=1, source_target_pairs={{0,16},{16,0},{1,17},{17,1},{2,18},{18,2},{3,19},{19,3},{4,20},{20... | collective-permute-start | bytes 393224 | tf_op jit(solution)/shard_map/ppermute | solution.py:269
  39.7 7.2 %collective-permute-start.18 = (f32[64,640]{1,0:T(8,128)S(1)}, f32[64,640]{1,0:T(8,128)S(1)}, u32[]{:S(2)}, u32[]{:S(2)}) collective-permute-start(f32[64,640]{1,0:T(8,128)S(1)} %get-tuple-element.130.own_ref), channel_id=1, source_target_pairs={{0,128},{128,0},{1,129},{129,1},{2,130},{130,2},{3,131},{131,3},{4... | collective-permute-start | bytes 491528 | tf_op jit(solution)/shard_map/ppermute | solution.py:269
  40.7 2.8 %collective-permute-start.17 = (f32[17,16,128]{2,1,0:T(8,128)S(1)}, f32[17,16,128]{2,1,0:T(8,128)S(1)}, u32[]{:S(2)}, u32[]{:S(2)}) collective-permute-start(f32[17,16,128]{2,1,0:T(8,128)S(1)} %get-tuple-element.163), channel_id=1, source_target_pairs={{0,16},{16,0},{1,17},{17,1},{2,18},{18,2},{3,19},{19,3},{4,20},{20... | collective-permute-start | bytes 417800 | tf_op jit(solution)/shard_map/ppermute | solution.py:269
  42.5 1.4 %collective-permute-start.16 = (f32[17,16,128]{2,1,0:T(8,128)S(1)}, f32[17,16,128]{2,1,0:T(8,128)S(1)}, u32[]{:S(2)}, u32[]{:S(2)}) collective-permute-start(f32[17,16,128]{2,1,0:T(8,128)S(1)} %get-tuple-element.164), channel_id=1, source_target_pairs={{0,16},{16,0},{1,17},{17,1},{2,18},{18,2},{3,19},{19,3},{4,20},{20... | collective-permute-start | bytes 417800 | tf_op jit(solution)/shard_map/ppermute | solution.py:269
  46.9 6.2 %collective-permute-start.19 = (f32[64,640]{1,0:T(8,128)S(1)}, f32[64,640]{1,0:T(8,128)S(1)}, u32[]{:S(2)}, u32[]{:S(2)}) collective-permute-start(f32[64,640]{1,0:T(8,128)S(1)} %shard_map.82.own_ref), channel_id=1, source_target_pairs={{0,128},{128,0},{1,129},{129,1},{2,130},{130,2},{3,131},{131,3},{4... | collective-permute-start | bytes 491528 | tf_op jit(solution)/shard_map/ppermute | solution.py:269
  50.2 4.7 %copy-start.2 = (f32[128,128]{1,0:T(8,128)S(1)}, f32[128,128]{1,0:T(8,128)}, u32[]{:S(2)}) copy-start(f32[128,128]{1,0:T(8,128)} %amp_ref.1) | copy-start | bytes 196612
  50.2 4.7 %copy-start.3 = (s32[2048]{0:T(1024)S(1)}, s32[2048]{0:T(1024)}, u32[]{:S(2)}) copy-start(s32[2048]{0:T(1024)} %param.13) | copy-start | bytes 24580
  50.2 4.7 %copy-start.4 = (f32[2048]{0:T(1024)S(1)}, f32[2048]{0:T(1024)}, u32[]{:S(2)}) copy-start(f32[2048]{0:T(1024)} %param.16) | copy-start | bytes 24580
  50.2 4.7 %copy-start.5 = (f32[640]{0:T(1024)S(1)}, f32[640]{0:T(1024)}, u32[]{:S(2)}) copy-start(f32[640]{0:T(1024)} %param.17) | copy-start | bytes 7684
  50.2 4.7 %copy-start.6 = (s32[128]{0:T(128)S(1)}, s32[128]{0:T(128)}, u32[]{:S(2)}) copy-start(s32[128]{0:T(128)} %param.14) | copy-start | bytes 1540
